TPU v7x, 128 devices: a whole 4x4x4 slice. The times are simulated.
128 devices in a mesh: gx: 8 (over y, core), yz: 16 (over z, x).
Axes of the slice: x: 4, y: 4, z: 4, core: 2. Of those that a mesh axis runs over, the one named last changes fastest.
Arguments:
- coeffs: bfloat16 [2048, 16, 256], P(('gx', 'yz')), may hold values from -6 to 6
- occupation: float32 [2048], P(('gx', 'yz')), may hold values from 0.5 to 2
- box_offset: int32 [2048, 3], P(('gx', 'yz')), may hold values from 0 to 496, as said below
- live_count: int32 [128], P(('gx', 'yz')), may hold values from 4 to 16, as said below
- synthesis: float32 [16, 16], replicated
- v_ext: float32 [192, 512, 128], P('gx', 'yz'), may hold values from -6 to 6
- core_density: float32 [192, 512, 128], P('gx', 'yz'), may hold values from 0.05 to 1
Outputs:
- hpsi: bfloat16 [2048, 16, 256], P(('gx', 'yz'))
- potential: float32 [192, 512, 128], P('gx', 'yz')
Inputs may be any that keep to these rules, and one draw needn't show every extreme that they name: `box_offset`: A function's box begins inside its owner's domain: the first coordinate lies in the owner's 24 planes along gx and the second in its 32 rows along yz; every box lies inside the grid. `live_count`: A device's used slots are its first ones; some device uses all 16.
All inputs are finite; a program needn't handle non-finite values.
Results may differ from a plain program's by a relative error of at most 0.001.
Values sent between devices are 32-bit elements; how exact they have to be, the bound alone decides.
A program may use at most 128 MiB of HBM per device.

v0:
```python
import jax
import jax.numpy as jnp
from jax import lax
from jax.sharding import PartitionSpec as P

XC_COEF = -0.9847450218426964


def passed_along(value, axis, steps):
    count = lax.axis_size(axis)
    first, last = (max(0, -steps), min(count, count - steps))
    return lax.ppermute(value, axis, [(source, source + steps) for source in range(first, last)])


def synthesize(values, synthesis):
    highest = lax.Precision.HIGHEST
    values = jnp.einsum("ai,fijk->fajk", synthesis, values, precision=highest)
    values = jnp.einsum("bj,fajk->fabk", synthesis, values, precision=highest)
    return jnp.einsum("ck,fabk->fabc", synthesis, values, precision=highest)


def analyze(values, synthesis):
    highest = lax.Precision.HIGHEST
    values = jnp.einsum("ai,fabc->fibc", synthesis, values, precision=highest)
    values = jnp.einsum("bj,fibc->fijc", synthesis, values, precision=highest)
    return jnp.einsum("ck,fijc->fijk", synthesis, values, precision=highest)


def footprint(offsets, rows_x, rows_y, depth_z, box_edge, width_y):
    steps = jnp.arange(box_edge, dtype=jnp.int32)
    local_x = offsets[:, 0] - lax.axis_index("gx") * rows_x
    local_y = offsets[:, 1] - lax.axis_index("yz") * rows_y
    place_x = local_x[:, None, None] + steps[None, :, None]
    place_y = local_y[:, None, None] + steps[None, None, :]
    lines = place_x * width_y + place_y
    inside = jnp.ones(lines.shape, jnp.float32)
    depth = jnp.arange(depth_z, dtype=jnp.int32)
    place_z = offsets[:, 2][:, None, None] + steps[None, :, None]
    onehot = (place_z == depth[None, None, :]).astype(jnp.float32)
    return (lines, inside, onehot)


def spread(weighted, inside, onehot):
    placed = jnp.einsum("fabc,fcz->fabz", weighted, onehot, precision=lax.Precision.HIGHEST)
    placed = placed * inside[:, :, :, None]
    return placed.reshape(-1, onehot.shape[2])


def collect(table, lines, inside, onehot):
    box_edge = onehot.shape[1]
    picked = table[lines.reshape(-1)].reshape(lines.shape[0], box_edge, box_edge, onehot.shape[2])
    values = jnp.einsum("fabz,fcz->fabc", picked, onehot, precision=lax.Precision.HIGHEST)
    return values * inside[:, :, :, None]


def shards(coeffs, occupation, box_offset, live_count, synthesis, v_ext, core_density):
    rows_x, rows_y, depth_z = v_ext.shape
    slot_count = coeffs.shape[0]
    box_edge = coeffs.shape[1]
    wide_x = rows_x + box_edge
    wide_y = rows_y + box_edge
    diagonal = lax.axis_size("yz") + 1
    blocks = coeffs.astype(jnp.float32).reshape(slot_count, box_edge, box_edge, box_edge)
    psi = synthesize(blocks, synthesis)
    slot = jnp.arange(slot_count, dtype=jnp.int32)
    live = (slot < live_count[0]).astype(jnp.float32)
    senders = occupation * live
    weighted = psi * psi * senders[:, None, None, None]
    lines, inside, onehot = footprint(box_offset, rows_x, rows_y, depth_z, box_edge, wide_y)
    buffer = jnp.zeros((wide_x * wide_y, depth_z), jnp.float32)
    buffer = (
        buffer.at[lines.reshape(-1)]
        .add(spread(weighted, inside, onehot))
        .reshape(wide_x, wide_y, depth_z)
    )
    from_x = passed_along(buffer[rows_x:, :rows_y], "gx", 1)
    from_y = passed_along(buffer[:rows_x, rows_y:], "yz", 1)
    from_corner = passed_along(buffer[rows_x:, rows_y:], ("gx", "yz"), diagonal)
    summed = buffer[:rows_x, :rows_y]
    summed = summed.at[:box_edge].add(from_x)
    summed = summed.at[:, :box_edge].add(from_y)
    summed = summed.at[:box_edge, :box_edge].add(from_corner)
    density = core_density + summed
    potential = v_ext + XC_COEF * jnp.cbrt(density)
    upper_x = passed_along(potential[:box_edge], "gx", -1)
    upper_y = passed_along(potential[:, :box_edge], "yz", -1)
    upper_corner = passed_along(potential[:box_edge, :box_edge], ("gx", "yz"), -diagonal)
    near_rows = jnp.concatenate([potential, upper_y], axis=1)
    far_rows = jnp.concatenate([upper_x, upper_corner], axis=1)
    extended = jnp.concatenate([near_rows, far_rows], axis=0)
    values = collect(extended.reshape(wide_x * wide_y, depth_z), lines, inside, onehot)
    applied = analyze(values * psi, synthesis) * live[:, None, None, None]
    hpsi = applied.astype(jnp.bfloat16).reshape(slot_count, box_edge, box_edge * box_edge)
    return (hpsi, potential)


def solution(mesh):
    placed = (
        P(("gx", "yz"), None, None),
        P(("gx", "yz")),
        P(("gx", "yz"), None),
        P(("gx", "yz")),
        P(),
        P("gx", "yz", None),
        P("gx", "yz", None),
    )
    return jax.shard_map(
        shards,
        mesh=mesh,
        in_specs=placed,
        out_specs=(P(("gx", "yz"), None, None), P("gx", "yz", None)),
        check_vma=False,
    )
```

profile of v0, /device:TPU:1, one launch (start us, length us, event | category | flops | bytes accessed | tf_op | source)
XLA Modules:
  0.0 127.5 jit_solution(16682804186068773672)
XLA Ops:
  1.3 0.8 slice_bitcast_fusion
  2.1 0.1 add_multiply_fusion
  2.2 0.1 iota_add_fusion
  2.2 0.1 broadcast_add_fusion
  2.4 0.1 add.127
  2.5 1.4 %copy.15 = bf16[16,16,256]{1,2,0:T(8,128)(2,1)S(1)} copy(bf16[16,16,256]{2,1,0:T(8,128)(2,1)} %param.13) | data formatting | bytes 262144 | tf_op jit(solution)/shard_map/reshape | solution.py:63
  3.9 1.0 convolution_bitcast_fusion
  4.9 2.4 %copy.11 = f32[16,16,16,16]{2,3,1,0:T(8,128)} copy(f32[16,16,16,16]{1,3,2,0:T(8,128)S(1)} %convolution_bitcast_fusion) | data formatting | bytes 524288 | tf_op jit(solution)/shard_map/ai,fijk->fajk/transpose | solution.py:17
  7.2 16.3 %fusion.29 = f32[16,16,16,16]{2,3,1,0:T(8,128)S(1)} fusion(f32[16,16,16,16]{2,3,1,0:T(8,128)} %copy.11, f32[16,16]{1,0:T(8,128)S(1)} %copy-done), kind=kOutput, calls=%fused_computation.37 | convolution fusion | flops 12582912 | bytes 525312 | tf_op jit(solution)/shard_map/bj,fajk->fabk/dot_general | solution.py:18
  23.6 1.8 %fusion.2 = f32[16,16,16,16]{3,2,1,0:T(8,128)S(1)} fusion(f32[16,16,16,16]{2,3,1,0:T(8,128)S(1)} %fusion.29, f32[16,16]{1,0:T(8,128)S(1)} %copy-done), kind=kOutput, calls=%fused_computation.4 | convolution fusion | flops 12582912 | bytes 525312 | tf_op jit(solution)/shard_map/ck,fabk->fabc/dot_general | solution.py:19
  25.4 2.6 %fusion.6 = f32[16,16,16,128]{3,2,1,0:T(8,128)} fusion(f32[16,16,16,16]{3,2,1,0:T(8,128)S(1)} %fusion.2, f32[16]{0:T(128)S(1)} %compare_select_fusion.1, s32[16,16]{1,0:T(8,128)S(1)} %get-tuple-element.43), kind=kOutput, calls=%fused_computation.9 | convolution fusion | flops 100827136 | bytes 2360384 | tf_op jit(solution)/shard_map/fabc,fcz->fabz/dot_general | solution.py:44
  28.1 22.9 %scatter_custom_fusion = f32[1920,128]{1,0:T(8,128)S(1)} fusion(s32[4096]{0:T(1024)S(1)} %bitcast.63, f32[4096,128]{1,0:T(8,128)} %bitcast.62, f32[]{:T(128)} %constant.94.clone.1), kind=kCustom, calls=%fused_computation.17 | custom fusion | flops 524288 | bytes 983552 | tf_op jit(solution)/shard_map/scatter-add | solution.py:73
  51.0 4.7 %collective-permute-start = (f32[16,32,128]{2,1,0:T(8,128)S(1)}, f32[16,32,128]{2,1,0:T(8,128)S(1)}, u32[]{:S(2)}, u32[]{:S(2)}) collective-permute-start(f32[16,32,128]{2,1,0:T(8,128)S(1)} %slice.128), channel_id=1, source_target_pairs={{0,16},{16,32},{32,48},{48,64},{64,80},{80,96},{96,112},{1,17},{17... | collective-permute-start | bytes 786440 | tf_op jit(solution)/shard_map/ppermute | solution.py:12
  55.8 2.8 %collective-permute-start.2 = (f32[16,16,128]{2,1,0:T(8,128)S(1)}, f32[16,16,128]{2,1,0:T(8,128)S(1)}, u32[]{:S(2)}, u32[]{:S(2)}) collective-permute-start(f32[16,16,128]{2,1,0:T(8,128)S(1)} %slice.132), channel_id=1, source_target_pairs={{0,17},{1,18},{2,19},{3,20},{4,21},{5,22},{6,23},{7,24},{8,25},{9,... | collective-permute-start | bytes 393224 | tf_op jit(solution)/shard_map/ppermute | solution.py:12
  58.6 3.3 %collective-permute-start.1 = (f32[24,16,128]{2,1,0:T(8,128)S(1)}, f32[24,16,128]{2,1,0:T(8,128)S(1)}, u32[]{:S(2)}, u32[]{:S(2)}) collective-permute-start(f32[24,16,128]{2,1,0:T(8,128)S(1)} %slice.130), channel_id=1, source_target_pairs={{0,1},{1,2},{2,3},{3,4},{4,5},{5,6},{6,7},{7,8},{8,9},{9,10},{10,1... | collective-permute-start | bytes 589832 | tf_op jit(solution)/shard_map/ppermute | solution.py:12
  62.1 3.3 %collective-permute-done.1 = f32[24,16,128]{2,1,0:T(8,128)S(1)} collective-permute-done((f32[24,16,128]{2,1,0:T(8,128)S(1)}, f32[24,16,128]{2,1,0:T(8,128)S(1)}, u32[]{:S(2)}, u32[]{:S(2)}) %collective-permute-start.1) | collective-permute-done | bytes 196640 | tf_op jit(solution)/shard_map/ppermute | solution.py:12
  65.3 0.1 constant_dynamic-update-slice_fusion
  65.5 0.3 multiply_add_fusion
  65.9 1.3 %collective-permute-start.5 = (f32[16,16,128]{2,1,0:T(8,128)S(1)}, f32[16,16,128]{2,1,0:T(8,128)S(1)}, u32[]{:S(2)}, u32[]{:S(2)}) collective-permute-start(f32[16,16,128]{2,1,0:T(8,128)S(1)} %slice.135), channel_id=1, source_target_pairs={{17,0},{18,1},{19,2},{20,3},{21,4},{22,5},{23,6},{24,7},{25,8},{26... | collective-permute-start | bytes 393224 | tf_op jit(solution)/shard_map/ppermute | solution.py:12
  67.2 1.3 %collective-permute-start.3 = (f32[24,16,128]{2,1,0:T(8,128)S(1)}, f32[24,16,128]{2,1,0:T(8,128)S(1)}, u32[]{:S(2)}, u32[]{:S(2)}) collective-permute-start(f32[24,16,128]{2,1,0:T(8,128)S(1)} %slice.133), channel_id=1, source_target_pairs={{1,0},{2,1},{3,2},{4,3},{5,4},{6,5},{7,6},{8,7},{9,8},{10,9},{11,1... | collective-permute-start | bytes 589832 | tf_op jit(solution)/shard_map/ppermute | solution.py:12
  68.5 3.4 %collective-permute-start.4 = (f32[16,32,128]{2,1,0:T(8,128)S(1)}, f32[16,32,128]{2,1,0:T(8,128)S(1)}, u32[]{:S(2)}, u32[]{:S(2)}) collective-permute-start(f32[16,32,128]{2,1,0:T(8,128)S(1)} %slice.134), channel_id=1, source_target_pairs={{16,0},{32,16},{48,32},{64,48},{80,64},{96,80},{112,96},{17,1},{33... | collective-permute-start | bytes 786440 | tf_op jit(solution)/shard_map/ppermute | solution.py:12
  72.0 3.5 %collective-permute-done.5 = f32[16,16,128]{2,1,0:T(8,128)S(1)} collective-permute-done((f32[16,16,128]{2,1,0:T(8,128)S(1)}, f32[16,16,128]{2,1,0:T(8,128)S(1)}, u32[]{:S(2)}, u32[]{:S(2)}) %collective-permute-start.5) | collective-permute-done | bytes 131104 | tf_op jit(solution)/shard_map/ppermute | solution.py:12
  75.5 2.3 %collective-permute-done.3 = f32[24,16,128]{2,1,0:T(8,128)S(1)} collective-permute-done((f32[24,16,128]{2,1,0:T(8,128)S(1)}, f32[24,16,128]{2,1,0:T(8,128)S(1)}, u32[]{:S(2)}, u32[]{:S(2)}) %collective-permute-start.3) | collective-permute-done | bytes 196640 | tf_op jit(solution)/shard_map/ppermute | solution.py:12
  77.7 6.8 %collective-permute-done.4 = f32[16,32,128]{2,1,0:T(8,128)S(1)} collective-permute-done((f32[16,32,128]{2,1,0:T(8,128)S(1)}, f32[16,32,128]{2,1,0:T(8,128)S(1)}, u32[]{:S(2)}, u32[]{:S(2)}) %collective-permute-start.4) | collective-permute-done | bytes 262176 | tf_op jit(solution)/shard_map/ppermute | solution.py:12
  84.6 0.1 maximum_maximum_fusion
  84.6 14.1 %gather_fusion = f32[4096,128]{1,0:T(8,128)} fusion(f32[1920,128]{1,0:T(8,128)S(1)} %bitcast.54, s32[4096]{0:T(1024)S(1)} %broadcast_clamp_fusion), kind=kCustom, calls=%fused_computation | custom fusion | bytes 4210688 | tf_op jit(solution)/shard_map/gather | solution.py:51
  98.7 2.8 %convolution_multiply_fusion = f32[16,16,16,16]{3,2,1,0:T(8,128)S(1)} fusion(f32[16,16,16,16]{3,2,1,0:T(8,128)S(1)} %fusion.2, f32[16,16,16,128]{3,2,1,0:T(8,128)} %bitcast.55, s32[16,16]{1,0:T(8,128)S(1)} %get-tuple-element.43), kind=kOutput, calls=%fused_computation.13 | convolution fusion | flops 100761600 | bytes 2622464 | tf_op jit(solution)/shard_map/fabz,fcz->fabc/dot_general | solution.py:52
  101.5 3.9 %fusion.9 = f32[16,16,16,16]{1,3,2,0:T(8,128)S(1)} fusion(f32[16,16,16,16]{3,2,1,0:T(8,128)S(1)} %convolution_multiply_fusion, f32[16,16]{1,0:T(8,128)S(1)} %copy-done), kind=kOutput, calls=%fused_computation.12 | convolution fusion | flops 12582912 | bytes 525312 | tf_op jit(solution)/shard_map/ai,fabc->fibc/dot_general | solution.py:24
  105.4 2.4 %copy.14 = f32[16,16,16,16]{2,3,1,0:T(8,128)} copy(f32[16,16,16,16]{1,3,2,0:T(8,128)S(1)} %fusion.9) | data formatting | bytes 524288 | tf_op jit(solution)/shard_map/ai,fabc->fibc/transpose | solution.py:24
  107.8 16.3 %fusion.25 = f32[16,16,16,16]{2,3,1,0:T(8,128)S(1)} fusion(f32[16,16,16,16]{2,3,1,0:T(8,128)} %copy.14, f32[16,16]{1,0:T(8,128)S(1)} %copy-done), kind=kOutput, calls=%fused_computation.33 | convolution fusion | flops 12582912 | bytes 525312 | tf_op jit(solution)/shard_map/bj,fibc->fijc/dot_general | solution.py:25
  124.1 1.8 %multiply_convert_fusion = bf16[16,16,16,16]{3,2,1,0:T(8,128)(2,1)S(1)} fusion(f32[16,16,16,16]{2,3,1,0:T(8,128)S(1)} %fusion.25, f32[16]{0:T(128)S(1)} %compare_convert_fusion, f32[16,16]{1,0:T(8,128)S(1)} %copy-done), kind=kOutput, calls=%fused_computation.8 | convolution fusion | flops 12713984 | bytes 394304 | tf_op jit(solution)/shard_map/ck,fijc->fijk/dot_general | solution.py:26
  125.9 1.7 %reshape.248 = bf16[16,16,256]{2,1,0:T(8,128)(2,1)} reshape(bf16[16,16,16,16]{3,2,1,0:T(8,128)(2,1)S(1)} %multiply_convert_fusion) | data formatting | bytes 262144 | tf_op jit(solution)/shard_map/reshape | solution.py:93
  (25 shorter events, 0.3 us)
Async XLA Ops:
  0.6 3.3 %copy-start = (f32[16,16]{1,0:T(8,128)S(1)}, f32[16,16]{1,0:T(8,128)}, u32[]{:S(2)}) copy-start(f32[16,16]{1,0:T(8,128)} %param.17) | copy-start | bytes 3076
  23.6 1.9 %copy-start.4 = (f32[16]{0:T(128)S(1)}, f32[16]{0:T(128)}, u32[]{:S(2)}) copy-start(f32[16]{0:T(128)} %param.14) | copy-start | bytes 196
  51.0 14.5 %copy-start.2 = (f32[24,32,128]{2,1,0:T(8,128)S(1)}, f32[24,32,128]{2,1,0:T(8,128)}, u32[]{:S(2)}) copy-start(f32[24,32,128]{2,1,0:T(8,128)} %param.18) | copy-start | bytes 1179652
  51.0 14.5 %copy-start.3 = (f32[24,32,128]{2,1,0:T(8,128)S(1)}, f32[24,32,128]{2,1,0:T(8,128)}, u32[]{:S(2)}) copy-start(f32[24,32,128]{2,1,0:T(8,128)} %param.19) | copy-start | bytes 1179652
  51.0 11.0 %collective-permute-start = (f32[16,32,128]{2,1,0:T(8,128)S(1)}, f32[16,32,128]{2,1,0:T(8,128)S(1)}, u32[]{:S(2)}, u32[]{:S(2)}) collective-permute-start(f32[16,32,128]{2,1,0:T(8,128)S(1)} %slice.128), channel_id=1, source_target_pairs={{0,16},{16,32},{32,48},{48,64},{64,80},{80,96},{96,112},{1,17},{17... | collective-permute-start | bytes 786440 | tf_op jit(solution)/shard_map/ppermute | solution.py:12
  55.8 9.6 %collective-permute-start.2 = (f32[16,16,128]{2,1,0:T(8,128)S(1)}, f32[16,16,128]{2,1,0:T(8,128)S(1)}, u32[]{:S(2)}, u32[]{:S(2)}) collective-permute-start(f32[16,16,128]{2,1,0:T(8,128)S(1)} %slice.132), channel_id=1, source_target_pairs={{0,17},{1,18},{2,19},{3,20},{4,21},{5,22},{6,23},{7,24},{8,25},{9,... | collective-permute-start | bytes 393224 | tf_op jit(solution)/shard_map/ppermute | solution.py:12
  58.6 6.7 %collective-permute-start.1 = (f32[24,16,128]{2,1,0:T(8,128)S(1)}, f32[24,16,128]{2,1,0:T(8,128)S(1)}, u32[]{:S(2)}, u32[]{:S(2)}) collective-permute-start(f32[24,16,128]{2,1,0:T(8,128)S(1)} %slice.130), channel_id=1, source_target_pairs={{0,1},{1,2},{2,3},{3,4},{4,5},{5,6},{6,7},{7,8},{8,9},{9,10},{10,1... | collective-permute-start | bytes 589832 | tf_op jit(solution)/shard_map/ppermute | solution.py:12
  65.8 32.9 %copy-start.1 = (f32[24,32,128]{2,1,0:T(8,128)}, f32[24,32,128]{2,1,0:T(8,128)S(1)}, u32[]{:S(2)}) copy-start(f32[24,32,128]{2,1,0:T(8,128)S(1)} %multiply_add_fusion) | copy-start | bytes 1179652
  65.9 9.5 %collective-permute-start.5 = (f32[16,16,128]{2,1,0:T(8,128)S(1)}, f32[16,16,128]{2,1,0:T(8,128)S(1)}, u32[]{:S(2)}, u32[]{:S(2)}) collective-permute-start(f32[16,16,128]{2,1,0:T(8,128)S(1)} %slice.135), channel_id=1, source_target_pairs={{17,0},{18,1},{19,2},{20,3},{21,4},{22,5},{23,6},{24,7},{25,8},{26... | collective-permute-start | bytes 393224 | tf_op jit(solution)/shard_map/ppermute | solution.py:12
  67.2 10.5 %collective-permute-start.3 = (f32[24,16,128]{2,1,0:T(8,128)S(1)}, f32[24,16,128]{2,1,0:T(8,128)S(1)}, u32[]{:S(2)}, u32[]{:S(2)}) collective-permute-start(f32[24,16,128]{2,1,0:T(8,128)S(1)} %slice.133), channel_id=1, source_target_pairs={{1,0},{2,1},{3,2},{4,3},{5,4},{6,5},{7,6},{8,7},{9,8},{10,9},{11,1... | collective-permute-start | bytes 589832 | tf_op jit(solution)/shard_map/ppermute | solution.py:12
  68.5 16.1 %collective-permute-start.4 = (f32[16,32,128]{2,1,0:T(8,128)S(1)}, f32[16,32,128]{2,1,0:T(8,128)S(1)}, u32[]{:S(2)}, u32[]{:S(2)}) collective-permute-start(f32[16,32,128]{2,1,0:T(8,128)S(1)} %slice.134), channel_id=1, source_target_pairs={{16,0},{32,16},{48,32},{64,48},{80,64},{96,80},{112,96},{17,1},{33... | collective-permute-start | bytes 786440 | tf_op jit(solution)/shard_map/ppermute | solution.py:12
where the time goes:
time: 128 us
  matrix products  46.5 us (36%)
  other arithmetic  24.5 us (19%)
  local copies, waits for them, and re-layouts  22.1 us (17%)
  starting transfers between devices  16.9 us (13%)
  waiting for transfers between devices  15.8 us (12%)
  between operations  1.6 us (1%)
    scatter-add x1, other arithmetic, shards(): buffer = buffer.at[lines.reshape(-1)].add(spread(weighted, inside, onehot...  22.9 us
    ppermute x6, starting transfers between devices, passed_along(): lax.ppermute(value, axis, [(source, source + steps) for source in range(f...  16.9 us
    dot_general x1, matrix products, synthesize(): values = jnp.einsum('bj,fajk->fabk', synthesis, values, precision=highest)  16.3 us
    dot_general x1, matrix products, analyze(): values = jnp.einsum('bj,fibc->fijc', synthesis, values, precision=highest)  16.3 us
    ppermute x6, waiting for transfers between devices, passed_along(): lax.ppermute(value, axis, [(source, source + steps) for source in range(f...  15.8 us
    gather x1, local copies, waits for them, and re-layouts, collect(): table[lines.reshape(-1)]  14.1 us
    dot_general x1, matrix products, analyze(): values = jnp.einsum('ai,fabc->fibc', synthesis, values, precision=highest)  3.89 us
    dot_general x1, matrix products, collect(): jnp.einsum('fabz,fcz->fabc', picked, onehot, precision=lax.Precision.HIGH...  2.78 us
  transfers between devices with their start and end apart: 6, of which 4 were waited for; matrix products, arithmetic and copies ran while one was open for 0% of the time, Pallas kernels for 0%

commit v1 on v0

v1 whole, which is shorter than its diff:
```python
import functools

import jax
import jax.numpy as jnp
from jax import lax
from jax.experimental import pallas as pl
from jax.experimental.pallas import tpu as pltpu
from jax.sharding import PartitionSpec as P

XC_COEF = -0.9847450218426964
EDGE = 16
CUBE = EDGE * EDGE
REACH = EDGE - 1
PAIR = 2
GROUP = 3
F32 = jnp.float32
BF16 = jnp.bfloat16
HIGHEST = lax.Precision.HIGHEST
MESH = pl.DeviceIdType.MESH


def iota(shape, dim):
    return lax.broadcasted_iota(jnp.int32, shape, dim)


def split(value):
    high = value.astype(BF16)
    low = (value - high.astype(F32)).astype(BF16)
    return high, low


def dot(left, right):
    return lax.dot_general(left, right, (((1,), (0,)), ((), ())), preferred_element_type=F32)


def dot_nt(left, right):
    return lax.dot_general(left, right, (((1,), (1,)), ((), ())), preferred_element_type=F32)


def swap_in_blocks(value):
    halves = []
    for half in range(CUBE // 128):
        part = value[:, half * 128 : (half + 1) * 128].reshape(CUBE // 8, 8, 128)
        row, col = iota(part.shape, 1), iota(part.shape, 2)
        for step in (1, 2, 4):
            up = pltpu.roll(pltpu.roll(part, 8 - step, 1), step, 2)
            down = pltpu.roll(pltpu.roll(part, step, 1), 128 - step, 2)
            moved = jnp.where((row & step) != 0, down, up)
            part = jnp.where(((row ^ col) & step) == 0, part, moved)
        part = part.reshape(EDGE, 2, 8, 128)
        first, second = part[:, 0], part[:, 1]
        far = (iota(first.shape, 2) & 8) != 0
        new_first = jnp.where(far, pltpu.roll(second, 8, 2), first)
        new_second = jnp.where(far, second, pltpu.roll(first, 120, 2))
        halves.append(jnp.stack([new_first, new_second], axis=1).reshape(CUBE, 128))
    return jnp.concatenate(halves, axis=1)


def kernel(
    sizes,
    occ_ref, off_ref, live_ref, syn_ref, coef_hbm, vext_hbm, core_hbm,
    hpsi_ref, pot_hbm,
    coef, vext, core, swapped, kron_hi, kron_lo, filt, psi, padded, partial, from_x, from_y, from_c, ext, back,
    in_sems, out_sems, send1, recv1, send2, recv2,
):
    slots, rows_x, rows_y, depth, n_gx, n_yz = sizes
    gx, yz = lax.axis_index("gx"), lax.axis_index("yz")
    wide_y = rows_y + EDGE
    stride = wide_y

    def corner(f):
        x = jnp.clip(off_ref[f, 0] - gx * rows_x, 0, rows_x - 1)
        y = jnp.clip(off_ref[f, 1] - yz * rows_y, 0, rows_y - 1)
        return x, y

    pairs = slots // PAIR

    copy_coef = pltpu.make_async_copy(coef_hbm, coef, in_sems.at[0])
    copy_vext = pltpu.make_async_copy(vext_hbm, vext, in_sems.at[1])
    copy_core = pltpu.make_async_copy(core_hbm, core, in_sems.at[2])
    copy_coef.start()
    copy_core.start()
    copy_vext.start()

    next_x, next_y = lax.rem(gx + 1, n_gx), lax.rem(yz + 1, n_yz)
    last_x, last_y = lax.rem(gx + n_gx - 1, n_gx), lax.rem(yz + n_yz - 1, n_yz)
    barrier = pltpu.get_barrier_semaphore()
    for device in (
        (next_x, yz), (last_x, yz), (gx, next_y), (gx, last_y), (next_x, next_y), (last_x, last_y),
    ):
        pl.semaphore_signal(barrier, inc=1, device_id=device, device_id_type=MESH)

    def clear(slot, carry):
        for plane in range(EDGE + 3):
            padded[slot, pl.ds(stride * plane, rows_y), :] = jnp.zeros((rows_y, depth), F32)
        for plane in (0, EDGE + 1):
            padded[slot, pl.ds(stride * plane + rows_y, EDGE), :] = jnp.zeros((EDGE, depth), F32)
        return carry

    lax.fori_loop(0, slots, clear, 0)

    syn = syn_ref[...]
    lane = iota((EDGE, CUBE), 1)
    row = iota((EDGE, CUBE), 0)
    by_i = lax.dot(syn, (lane % EDGE == row).astype(F32), precision=HIGHEST, preferred_element_type=F32)
    by_j = lax.dot(syn, (lane // EDGE == row).astype(F32), precision=HIGHEST, preferred_element_type=F32)
    for a in range(EDGE):
        high, low = split(by_i[a : a + 1, :] * by_j)
        kron_hi[a * EDGE : (a + 1) * EDGE, :] = high
        kron_lo[a * EDGE : (a + 1) * EDGE, :] = low

    shift = iota((EDGE, depth), 1) - iota((EDGE, depth), 0)
    places = jnp.concatenate([(shift == off_ref[f, 2]).astype(F32) for f in range(slots)], axis=1)
    placed = lax.dot_general(syn, places, (((0,), (0,)), ((), ())), precision=HIGHEST, preferred_element_type=F32)
    placed_hi, placed_lo = split(placed)
    nothing = jnp.zeros((EDGE, depth), BF16)
    for pair in range(pairs):
        for piece, source in enumerate((placed_hi, placed_hi, placed_lo)):
            for h in range(PAIR):
                f = pair * PAIR + h
                at = (piece * PAIR + h) * EDGE
                for lanes in range(PAIR):
                    what = source[:, f * depth : (f + 1) * depth] if lanes == h else nothing
                    filt[pair, at : at + EDGE, lanes * depth : (lanes + 1) * depth] = what

    copy_coef.wait()
    swapped[...] = swap_in_blocks(coef[...].reshape(slots * EDGE, CUBE).astype(F32)).astype(BF16)

    span = PAIR * EDGE

    def synthesize(pair, carry):
        part = swapped[pl.ds(pl.multiple_of(pair * span, span), span), :]
        part = jnp.concatenate([part, part, part], axis=0)
        inner = dot_nt(kron_hi[...], part) + dot_nt(kron_lo[...], part)
        high = inner.astype(BF16).astype(F32)
        where = iota(inner.shape, 1)
        packed = jnp.where((where >= span) & (where < 2 * span), inner - high, high).astype(BF16)
        values = dot(packed, filt[pair])
        for h in range(PAIR):
            f = pair * PAIR + h
            value = values[:, h * depth : (h + 1) * depth]
            psi[f] = value
            weight = jnp.where(f < live_ref[0], occ_ref[f], 0.0)
            square = value * value * weight
            for a in range(EDGE):
                padded[f, pl.ds(stride * (a + 1) + rows_y, EDGE), :] = square[a * EDGE : (a + 1) * EDGE, :]
        return carry

    lax.fori_loop(0, pairs, synthesize, 0)

    def sum_plane(x):
        total = jnp.zeros((wide_y, depth), F32)
        for f in range(slots):
            corner_x, corner_y = corner(f)
            start = jnp.clip(x - corner_x + 1, 0, EDGE + 1) * stride + rows_y - corner_y
            total = total + padded[f, pl.ds(start, wide_y), :]
        partial[x] = total

    def sum_planes(first, count):
        def body(step, carry):
            sum_plane(first + step)
            return carry

        lax.fori_loop(0, count, body, 0)

    groups = REACH // GROUP
    all_groups = rows_x // GROUP

    def send(src, dst, sends, recvs, index, device):
        return pltpu.make_async_remote_copy(
            src_ref=src, dst_ref=dst, send_sem=sends.at[index], recv_sem=recvs.at[index],
            device_id=device, device_id_type=MESH,
        )

    first = {}
    for g in range(all_groups):
        here = pl.ds(g * GROUP, GROUP)
        if g < groups:
            there = pl.ds(rows_x + g * GROUP, GROUP)
            sum_planes(rows_x + g * GROUP, GROUP)
        sum_planes(g * GROUP, GROUP)
        if g == 0:
            pl.semaphore_wait(barrier, 6)
        copies = [send(partial.at[here, pl.ds(rows_y, EDGE)], from_y.at[here], send1, recv1, 3 * g, (gx, next_y))]
        if g < groups:
            copies.append(send(
                partial.at[there, pl.ds(rows_y, EDGE)], from_c.at[here], send1, recv1, 3 * g + 1, (next_x, next_y)))
            copies.append(send(
                partial.at[there, pl.ds(0, rows_y)], from_x.at[here], send1, recv1, 3 * g + 2, (next_x, yz)))
        for copy in copies:
            copy.start()
        first[g] = copies

    copy_core.wait()
    copy_vext.wait()

    second = {}
    out_copies = []
    for g in range(all_groups):
        here = pl.ds(g * GROUP, GROUP)
        for copy in first[g]:
            copy.wait_recv()
        density = core[here] + partial[here, pl.ds(0, rows_y), :]
        if g < groups:
            density = density + from_x[here]
            edge = density[:, :EDGE] + (from_y[here] + from_c[here])
        else:
            edge = density[:, :EDGE] + from_y[here]
        density = jnp.concatenate([edge, density[:, EDGE:]], axis=1)
        ext[here, pl.ds(0, rows_y), :] = vext[here] + XC_COEF * jnp.exp2(jnp.log2(density) * (1.0 / 3.0))
        copies = [send(ext.at[here, pl.ds(0, EDGE)], ext.at[here, pl.ds(rows_y, EDGE)], send2, recv2, 3 * g, (gx, last_y))]
        if g < groups:
            there = pl.ds(rows_x + g * GROUP, GROUP)
            copies.append(send(
                ext.at[here, pl.ds(0, EDGE)], ext.at[there, pl.ds(rows_y, EDGE)], send2, recv2, 3 * g + 1,
                (last_x, last_y)))
            copies.append(send(
                ext.at[here, pl.ds(0, rows_y)], ext.at[there, pl.ds(0, rows_y)], send2, recv2, 3 * g + 2, (last_x, yz)))
        for copy in copies:
            copy.start()
        second[g] = copies
        out = pltpu.make_async_copy(ext.at[here, pl.ds(0, rows_y)], pot_hbm.at[here], out_sems.at[g])
        out.start()
        out_copies.append(out)

    for g in range(all_groups):
        for copy in second[g]:
            copy.wait_recv()

    def analyze(pair, carry):
        parts = []
        for h in range(PAIR):
            f = pair * PAIR + h
            x, y = corner(f)
            box = ext[pl.ds(x, EDGE), pl.ds(y, EDGE), :].reshape(CUBE, depth)
            parts.append(box * psi[f])
        high, low = split(jnp.concatenate(parts, axis=1))
        left = filt[pair]
        both = dot_nt(left[span:], high)
        inner = both[:span] + both[span:] + dot_nt(left[:span], low)
        back[pl.ds(pl.multiple_of(pair * span, span), span), :] = inner
        return carry

    lax.fori_loop(0, pairs, analyze, 0)
    high, low = split(back[...])
    result = dot(high, kron_hi[...]) + (dot(high, kron_lo[...]) + dot(low, kron_hi[...]))
    result = swap_in_blocks(result)
    used = iota(result.shape, 0) < live_ref[0] * EDGE
    result = jnp.where(used, result, 0.0)
    hpsi_ref[...] = result.astype(BF16).reshape(slots, EDGE, CUBE)

    for g in range(all_groups):
        for copy in first[g] + second[g]:
            copy.wait_send()
        out_copies[g].wait()


def shards(n_gx, n_yz, coeffs, occupation, box_offset, live_count, synthesis, v_ext, core_density):
    slots = coeffs.shape[0]
    rows_x, rows_y, depth = v_ext.shape
    wide_x, wide_y = rows_x + EDGE, rows_y + EDGE
    exchanges = 3 * (rows_x // GROUP)
    smem = pl.BlockSpec(memory_space=pltpu.SMEM)
    vmem = pl.BlockSpec(memory_space=pltpu.VMEM)
    anywhere = pl.BlockSpec(memory_space=pl.ANY)
    return pl.pallas_call(
        functools.partial(kernel, (slots, rows_x, rows_y, depth, n_gx, n_yz)),
        out_shape=(
            jax.ShapeDtypeStruct(coeffs.shape, BF16),
            jax.ShapeDtypeStruct(v_ext.shape, F32),
        ),
        in_specs=[smem, smem, smem, vmem, anywhere, anywhere, anywhere],
        out_specs=(vmem, anywhere),
        scratch_shapes=[
            pltpu.VMEM(coeffs.shape, BF16),
            pltpu.VMEM(v_ext.shape, F32),
            pltpu.VMEM(v_ext.shape, F32),
            pltpu.VMEM((slots * EDGE, CUBE), BF16),
            pltpu.VMEM((CUBE, CUBE), BF16),
            pltpu.VMEM((CUBE, CUBE), BF16),
            pltpu.VMEM((slots // PAIR, 3 * PAIR * EDGE, PAIR * depth), BF16),
            pltpu.VMEM((slots, CUBE, depth), F32),
            pltpu.VMEM((slots, wide_y * (EDGE + 2) + rows_y, depth), F32),
            pltpu.VMEM((wide_x, wide_y, depth), F32),
            pltpu.VMEM((REACH, rows_y, depth), F32),
            pltpu.VMEM((rows_x, EDGE, depth), F32),
            pltpu.VMEM((REACH, EDGE, depth), F32),
            pltpu.VMEM((wide_x, wide_y, depth), F32),
            pltpu.VMEM((slots * EDGE, CUBE), F32),
            pltpu.SemaphoreType.DMA((3,)),
            pltpu.SemaphoreType.DMA((rows_x // GROUP,)),
            pltpu.SemaphoreType.DMA((exchanges,)),
            pltpu.SemaphoreType.DMA((exchanges,)),
            pltpu.SemaphoreType.DMA((exchanges,)),
            pltpu.SemaphoreType.DMA((exchanges,)),
        ],
        compiler_params=pltpu.CompilerParams(
            collective_id=0, has_side_effects=True, vmem_limit_bytes=40 * 1024 * 1024
        ),
    )(occupation, box_offset, live_count, synthesis, coeffs, v_ext, core_density)


def solution(mesh):
    placed = (
        P(("gx", "yz"), None, None),
        P(("gx", "yz")),
        P(("gx", "yz"), None),
        P(("gx", "yz")),
        P(),
        P("gx", "yz", None),
        P("gx", "yz", None),
    )
    return jax.shard_map(
        functools.partial(shards, mesh.shape["gx"], mesh.shape["yz"]),
        mesh=mesh,
        in_specs=placed,
        out_specs=(P(("gx", "yz"), None, None), P("gx", "yz", None)),
        check_vma=False,
    )
```

time: 128 us -> 33.2 us (0.26)
  matrix products: 46.5 us -> 0 us
  Pallas kernels: 0 us -> 26.6 us
  other arithmetic: 24.5 us -> 0 us
  local copies, waits for them, and re-layouts: 22.1 us -> 5.07 us
  starting transfers between devices: 16.9 us -> 0 us
  waiting for transfers between devices: 15.8 us -> 0 us
    dot_general x8 -> x0, matrix products: 46.5 us -> none  [the longest x1 16.3 us: synthesize(): values = jnp.einsum('bj,fajk->fabk', synthesis, values, precision=highest)]
    pallas_call x0 -> x1, Pallas kernels: none -> 26.6 us  [shards(): pl.pallas_call(functools.partial(kernel, (slots, rows_x, rows_y, depth, n...]
    scatter-add x4 -> x0, other arithmetic: 23 us -> none  [the longest x1 22.9 us: shards(): buffer = buffer.at[lines.reshape(-1)].add(spread(weighted, inside, onehot...]
    ppermute x6 -> x0, starting transfers between devices: 16.9 us -> none  [passed_along(): lax.ppermute(value, axis, [(source, source + steps) for source in range(f...]
    ppermute x6 -> x0, waiting for transfers between devices: 15.8 us -> none  [passed_along(): lax.ppermute(value, axis, [(source, source + steps) for source in range(f...]
    gather x1 -> x0, local copies, waits for them, and re-layouts: 14.1 us -> none  [collect(): table[lines.reshape(-1)]]
    unnamed x10 -> x13, local copies, waits for them, and re-layouts: 0.03 us -> 5.07 us
    transpose x2 -> x0, local copies, waits for them, and re-layouts: 4.75 us -> none  [the longest x1 2.37 us: analyze(): values = jnp.einsum('ai,fabc->fibc', synthesis, values, precision=highest)]
  transfers between devices with their start and end apart: 6 -> 0, of which waited for: 4 -> 0; matrix products, arithmetic and copies ran while one was open for 0% -> 0% of each run, Pallas kernels for 0% -> 0%
where the time goes in v1:
time: 33.2 us; the launch traced here: 33 us
  Pallas kernels  26.6 us (80%)
  local copies, waits for them, and re-layouts  5.07 us (15%)
  between operations  1.32 us (4%)
    pallas_call x1, Pallas kernels, shards(): pl.pallas_call(functools.partial(kernel, (slots, rows_x, rows_y, depth, n...  26.6 us
    unnamed x13, local copies, waits for them, and re-layouts  5.07 us

profile of v1, /device:TPU:1, one launch (start us, length us, event | category | flops | bytes accessed | tf_op | source)
XLA Modules:
  0.0 33.0 jit_solution(1984978943335538261)
XLA Ops:
  0.6 0.0 copy-start.3
  1.3 0.0 copy-start.4
  1.3 0.8 %copy.9.off_ref = s32[16,3]{1,0:T(8,128)S(1)} copy(s32[16,3]{0,1:T(4,128)} %param.9) | data formatting | bytes 384 | tf_op args[2]
  2.1 0.0 copy-done.3
  2.1 0.0 copy-done.4
  2.1 0.0 copy-start
  2.1 1.0 %copy-done = f32[24,32,128]{2,1,0:T(8,128)S(1)} copy-done((f32[24,32,128]{2,1,0:T(8,128)S(1)}, f32[24,32,128]{2,1,0:T(8,128)}, u32[]{:S(2)}) %copy-start) | copy-done | bytes 393240
  3.1 0.0 copy-start.1
  3.1 1.0 %copy-done.1 = f32[24,32,128]{2,1,0:T(8,128)S(1)} copy-done((f32[24,32,128]{2,1,0:T(8,128)S(1)}, f32[24,32,128]{2,1,0:T(8,128)}, u32[]{:S(2)}) %copy-start.1) | copy-done | bytes 393240
  4.1 0.0 copy-start.2
  4.1 0.9 %copy-done.2 = bf16[16,16,256]{2,1,0:T(8,128)(2,1)S(1)} copy-done((bf16[16,16,256]{2,1,0:T(8,128)(2,1)S(1)}, bf16[16,16,256]{2,1,0:T(8,128)(2,1)}, u32[]{:S(2)}) %copy-start.2) | copy-done | bytes 131096
  5.0 26.6 %shard_map.86 = (bf16[16,16,256]{2,1,0:T(8,128)(2,1)S(1)}, f32[24,32,128]{2,1,0:T(8,128)S(1)}) custom-call(f32[16]{0:T(128)S(1)} %copy-done.4, s32[16,3]{1,0:T(8,128)S(1)} %copy.9.off_ref, s32[1]{0:T(128)S(6)} %copy.12.live_ref, f32[16,16]{1,0:T(8,128)S(1)} %copy-done.3, bf16[16,16,256]{2,1,0:T(8,128)(2,1)S(1)} %copy-done.2, f32[24,32,128]{2,1,0:T(8,128)S(1)} %copy-done, ...), custom_call_target="tpu_custom_call" | custom-call | tf_op jit(solution)/shard_map/pallas_call | solution.py:266
  31.6 0.7 %copy.13 = bf16[16,16,256]{2,1,0:T(8,128)(2,1)} copy(bf16[16,16,256]{2,1,0:T(8,128)(2,1)S(1)} %get-tuple-element.4) | data formatting | bytes 262144
  32.2 0.7 %copy.14 = f32[24,32,128]{2,1,0:T(8,128)} copy(f32[24,32,128]{2,1,0:T(8,128)S(1)} %get-tuple-element.5) | data formatting | bytes 786432
Async XLA Ops:
  0.6 1.4 %copy-start.3 = (f32[16,16]{1,0:T(8,128)S(1)}, f32[16,16]{1,0:T(8,128)}, u32[]{:S(2)}) copy-start(f32[16,16]{1,0:T(8,128)} %syn_ref.1) | copy-start | bytes 3076
  1.3 0.8 %copy-start.4 = (f32[16]{0:T(128)S(1)}, f32[16]{0:T(128)}, u32[]{:S(2)}) copy-start(f32[16]{0:T(128)} %occ_ref.1) | copy-start | bytes 196
  2.1 1.0 %copy-start = (f32[24,32,128]{2,1,0:T(8,128)S(1)}, f32[24,32,128]{2,1,0:T(8,128)}, u32[]{:S(2)}) copy-start(f32[24,32,128]{2,1,0:T(8,128)} %vext_hbm.1) | copy-start | bytes 1179652
  3.1 1.0 %copy-start.1 = (f32[24,32,128]{2,1,0:T(8,128)S(1)}, f32[24,32,128]{2,1,0:T(8,128)}, u32[]{:S(2)}) copy-start(f32[24,32,128]{2,1,0:T(8,128)} %core_hbm.1) | copy-start | bytes 1179652
  4.1 0.9 %copy-start.2 = (bf16[16,16,256]{2,1,0:T(8,128)(2,1)S(1)}, bf16[16,16,256]{2,1,0:T(8,128)(2,1)}, u32[]{:S(2)}) copy-start(bf16[16,16,256]{2,1,0:T(8,128)(2,1)} %coef_hbm.1) | copy-start | bytes 393220

commit v2 on v1

v2 whole, which is shorter than its diff:
```python
import functools

import jax
import jax.numpy as jnp
from jax import lax
from jax.experimental import pallas as pl
from jax.experimental.pallas import tpu as pltpu
from jax.sharding import PartitionSpec as P

XC_COEF = -0.9847450218426964
EDGE = 16
CUBE = EDGE * EDGE
REACH = EDGE - 1
PAIR = 4
GROUP = 5
F32 = jnp.float32
BF16 = jnp.bfloat16
HIGHEST = lax.Precision.HIGHEST
MESH = pl.DeviceIdType.MESH


def iota(shape, dim):
    return lax.broadcasted_iota(jnp.int32, shape, dim)


def split(value):
    high = value.astype(BF16)
    low = (value - high.astype(F32)).astype(BF16)
    return high, low


def dot(left, right):
    return lax.dot_general(left, right, (((1,), (0,)), ((), ())), preferred_element_type=F32)


def dot_nt(left, right):
    return lax.dot_general(left, right, (((1,), (1,)), ((), ())), preferred_element_type=F32)


def swap_in_blocks(value):
    halves = []
    for half in range(CUBE // 128):
        part = value[:, half * 128 : (half + 1) * 128].reshape(CUBE // 8, 8, 128)
        row, col = iota(part.shape, 1), iota(part.shape, 2)
        for step in (1, 2, 4):
            up = pltpu.roll(pltpu.roll(part, 8 - step, 1), step, 2)
            down = pltpu.roll(pltpu.roll(part, step, 1), 128 - step, 2)
            moved = jnp.where((row & step) != 0, down, up)
            part = jnp.where(((row ^ col) & step) == 0, part, moved)
        part = part.reshape(EDGE, 2, 8, 128)
        first, second = part[:, 0], part[:, 1]
        far = (iota(first.shape, 2) & 8) != 0
        new_first = jnp.where(far, pltpu.roll(second, 8, 2), first)
        new_second = jnp.where(far, second, pltpu.roll(first, 120, 2))
        halves.append(jnp.stack([new_first, new_second], axis=1).reshape(CUBE, 128))
    return jnp.concatenate(halves, axis=1)


def kernel(
    sizes,
    occ_hbm, off_hbm, live, syn_hbm, coef_hbm, vext_hbm, core_hbm,
    hpsi_ref, ext,
    occ, off, off_rows, syn_ref, coef, vext, core, start_rows, starts,
    swapped, kron_hi, kron_lo, filt, psi, padded, partial, from_x, from_y, back,
    in_sems, table_sem, send_sems, recv_sems,
):
    slots, rows_x, rows_y, depth, n_gx, n_yz = sizes
    gx, yz = lax.axis_index("gx"), lax.axis_index("yz")
    wide_y = rows_y + EDGE
    stride = wide_y
    pairs = slots // PAIR

    inputs = (
        (coef_hbm, coef), (off_hbm, off), (off_hbm, off_rows), (syn_hbm, syn_ref), (occ_hbm, occ),
        (core_hbm, core), (vext_hbm, vext),
    )
    loads = [pltpu.make_async_copy(src, dst, in_sems.at[n]) for n, (src, dst) in enumerate(inputs)]
    for load in loads:
        load.start()
    load_coef, load_off, load_off_rows, load_syn, load_occ, load_core, load_vext = loads

    after_x, before_x = gx < n_gx - 1, gx > 0
    after_y, before_y = yz < n_yz - 1, yz > 0
    next_x, next_y, last_x, last_y = (gx + 1, yz), (gx, yz + 1), (gx - 1, yz), (gx, yz - 1)
    barrier = pltpu.get_barrier_semaphore()
    neighbours = 0
    for there, device in ((after_x, next_x), (after_y, next_y), (before_x, last_x), (before_y, last_y)):
        @pl.when(there)
        def _(device=device):
            pl.semaphore_signal(barrier, inc=1, device_id=device, device_id_type=MESH)

        neighbours = neighbours + there.astype(jnp.int32)

    @pl.when(jnp.logical_not(before_x))
    def _():
        from_x[...] = jnp.zeros_like(from_x)

    @pl.when(jnp.logical_not(before_y))
    def _():
        from_y[...] = jnp.zeros_like(from_y)

    def clear(slot, carry):
        for plane in range(EDGE + 3):
            padded[slot, pl.ds(stride * plane, rows_y), :] = jnp.zeros((rows_y, depth), F32)
        for plane in (0, EDGE + 1):
            padded[slot, pl.ds(stride * plane + rows_y, EDGE), :] = jnp.zeros((EDGE, depth), F32)
        return carry

    lax.fori_loop(0, slots, clear, 0)

    load_off_rows.wait()
    begin_x = jnp.clip(off_rows[0:1, :] - gx * rows_x, 0, rows_x - 1)
    begin_y = jnp.clip(off_rows[1:2, :] - yz * rows_y, 0, rows_y - 1)
    plane = jnp.clip(iota((rows_x + EDGE, slots), 0) - begin_x + 1, 0, EDGE + 1)
    start_rows[:, :slots] = plane * stride + rows_y - begin_y
    table = pltpu.make_async_copy(start_rows, starts, table_sem)
    table.start()

    load_syn.wait()
    syn = syn_ref[...]
    lane = iota((EDGE, CUBE), 1)
    row = iota((EDGE, CUBE), 0)
    by_i = lax.dot(syn, (lane % EDGE == row).astype(F32), precision=HIGHEST, preferred_element_type=F32)
    by_j = lax.dot(syn, (lane // EDGE == row).astype(F32), precision=HIGHEST, preferred_element_type=F32)
    for a in range(EDGE):
        high, low = split(by_i[a : a + 1, :] * by_j)
        kron_hi[a * EDGE : (a + 1) * EDGE, :] = high
        kron_lo[a * EDGE : (a + 1) * EDGE, :] = low

    load_off.wait()
    load_occ.wait()
    shift = iota((EDGE, depth), 1) - iota((EDGE, depth), 0)
    places = jnp.concatenate([(shift == off[2, f]).astype(F32) for f in range(slots)], axis=1)
    placed = lax.dot_general(syn, places, (((0,), (0,)), ((), ())), precision=HIGHEST, preferred_element_type=F32)
    placed_hi, placed_lo = split(placed)
    nothing = jnp.zeros((EDGE, depth), BF16)
    for pair in range(pairs):
        for piece, source in enumerate((placed_hi, placed_hi, placed_lo)):
            for h in range(PAIR):
                f = pair * PAIR + h
                at = (piece * PAIR + h) * EDGE
                for lanes in range(PAIR):
                    what = source[:, f * depth : (f + 1) * depth] if lanes == h else nothing
                    filt[pair, at : at + EDGE, lanes * depth : (lanes + 1) * depth] = what

    def corner(f):
        x = jnp.clip(off[0, f] - gx * rows_x, 0, rows_x - 1)
        y = jnp.clip(off[1, f] - yz * rows_y, 0, rows_y - 1)
        return x, y

    load_coef.wait()
    swapped[...] = swap_in_blocks(coef[...].reshape(slots * EDGE, CUBE).astype(F32)).astype(BF16)

    span = PAIR * EDGE

    def synthesize(pair, carry):
        part = swapped[pl.ds(pl.multiple_of(pair * span, span), span), :]
        part = jnp.concatenate([part, part, part], axis=0)
        inner = dot_nt(kron_hi[...], part) + dot_nt(kron_lo[...], part)
        high = inner.astype(BF16).astype(F32)
        where = iota(inner.shape, 1)
        packed = jnp.where((where >= span) & (where < 2 * span), inner - high, high).astype(BF16)
        values = dot(packed, filt[pair])
        for h in range(PAIR):
            f = pair * PAIR + h
            value = values[:, h * depth : (h + 1) * depth]
            psi[f] = value
            weight = jnp.where(f < live[0], occ[f], 0.0)
            square = value * value * weight
            for a in range(EDGE):
                padded[f, pl.ds(stride * (a + 1) + rows_y, EDGE), :] = square[a * EDGE : (a + 1) * EDGE, :]
        return carry

    lax.fori_loop(0, pairs, synthesize, 0)

    def sum_planes(first, count, unit):
        def body(step, carry):
            x = first + step * unit
            totals = [None] * unit
            for f in range(slots):
                for n in range(unit):
                    rows = padded[f, pl.ds(starts[x + n, f], wide_y), :]
                    totals[n] = rows if f == 0 else totals[n] + rows
            for n in range(unit):
                partial[x + n] = totals[n]
            return carry

        lax.fori_loop(0, count // unit, body, 0)

    table.wait()
    issued = []

    def copy(there, src, dst, device, arrives):
        index = len(issued)
        descriptor = pltpu.make_async_remote_copy(
            src_ref=src, dst_ref=dst, send_sem=send_sems.at[index], recv_sem=recv_sems.at[index],
            device_id=device, device_id_type=MESH,
        )

        @pl.when(there)
        def _():
            descriptor.start()

        issued.append((there, descriptor))

        def landed():
            @pl.when(arrives)
            def _():
                descriptor.wait_recv()

        return landed

    groups = REACH // GROUP
    rest = rows_x - REACH
    near, far = pl.ds(0, rows_y), pl.ds(rows_y, EDGE)
    edge, inner = pl.ds(0, EDGE), pl.ds(EDGE, rows_y - EDGE)
    spans = [pl.ds(g * GROUP, GROUP) for g in range(groups)]
    beyond = [pl.ds(rows_x + g * GROUP, GROUP) for g in range(groups)]
    others = pl.ds(REACH, rest)

    corner_in, main_in, side_in = [], [], []
    for g in range(groups):
        sum_planes(rows_x + g * GROUP, GROUP, GROUP)
        if g == 0:
            pl.semaphore_wait(barrier, neighbours)
        corner_in.append(copy(after_x, partial.at[beyond[g], far], from_x.at[spans[g], far], next_x, before_x))
    sum_planes(REACH, rest, 3)
    rest_in = copy(after_y, partial.at[others, far], from_y.at[others], next_y, before_y)
    for g in range(groups):
        main_in.append(copy(after_x, partial.at[beyond[g], near], from_x.at[spans[g], near], next_x, before_x))
    sum_planes(0, REACH, GROUP)
    for g in range(groups):
        corner_in[g]()
        partial[spans[g], far, :] += from_x[spans[g], far, :]
        side_in.append(copy(after_y, partial.at[spans[g], far], from_y.at[spans[g]], next_y, before_y))

    def apply(planes, along_x, along_y):
        rows = edge if along_y else inner
        density = core[planes, rows, :] + partial[planes, rows, :]
        if along_x:
            density = density + from_x[planes, rows, :]
        if along_y:
            density = density + from_y[planes]
        ext[planes, rows, :] = vext[planes, rows, :] + XC_COEF * jnp.exp2(jnp.log2(density) * (1.0 / 3.0))

    load_core.wait()
    load_vext.wait()
    rest_in()
    apply(others, False, True)
    apply(others, False, False)
    waits = [copy(before_y, ext.at[others, edge], ext.at[others, far], last_y, after_y)]
    back_in = []
    for g in range(groups):
        main_in[g]()
        apply(spans[g], True, False)
        waits.append(copy(before_x, ext.at[spans[g], inner], ext.at[beyond[g], inner], last_x, after_x))
    for g in range(groups):
        side_in[g]()
        apply(spans[g], True, True)
        back_in.append(copy(before_y, ext.at[spans[g], edge], ext.at[spans[g], far], last_y, after_y))
        waits.append(copy(before_x, ext.at[spans[g], edge], ext.at[beyond[g], edge], last_x, after_x))
    for g in range(groups):
        back_in[g]()
        waits.append(copy(
            before_x & after_y, ext.at[spans[g], far], ext.at[beyond[g], far], last_x, after_x & after_y))
    for landed in waits:
        landed()

    def analyze(pair, carry):
        parts = []
        for h in range(PAIR):
            f = pair * PAIR + h
            x, y = corner(f)
            box = ext[pl.ds(x, EDGE), pl.ds(y, EDGE), :].reshape(CUBE, depth)
            parts.append(box * psi[f])
        high, low = split(jnp.concatenate(parts, axis=1))
        left = filt[pair]
        both = dot_nt(left[span:], high)
        inner = both[:span] + both[span:] + dot_nt(left[:span], low)
        back[pl.ds(pl.multiple_of(pair * span, span), span), :] = inner
        return carry

    lax.fori_loop(0, pairs, analyze, 0)
    high, low = split(back[...])
    result = dot(high, kron_hi[...]) + (dot(high, kron_lo[...]) + dot(low, kron_hi[...]))
    result = swap_in_blocks(result)
    used = iota(result.shape, 0) < live[0] * EDGE
    result = jnp.where(used, result, 0.0)
    hpsi_ref[...] = result.astype(BF16).reshape(slots, EDGE, CUBE)

    for there, descriptor in issued:
        @pl.when(there)
        def _(descriptor=descriptor):
            descriptor.wait_send()


def deliver(hpsi_ref, ext, hpsi_hbm, pot_hbm, sems):
    rows_x, rows_y, _ = pot_hbm.shape
    copies = (
        pltpu.make_async_copy(hpsi_ref, hpsi_hbm, sems.at[0]),
        pltpu.make_async_copy(ext.at[pl.ds(0, rows_x), pl.ds(0, rows_y)], pot_hbm, sems.at[1]),
    )
    for copy in copies:
        copy.start()
    for copy in copies:
        copy.wait()


def shards(n_gx, n_yz, coeffs, occupation, box_offset, live_count, synthesis, v_ext, core_density):
    slots = coeffs.shape[0]
    rows_x, rows_y, depth = v_ext.shape
    wide_x, wide_y = rows_x + EDGE, rows_y + EDGE
    exchanges = 2 + 7 * (REACH // GROUP)
    vmem = pl.BlockSpec(memory_space=pltpu.VMEM)
    hbm = pl.BlockSpec(memory_space=pltpu.HBM)
    inputs = (occupation, box_offset.T, live_count, synthesis, coeffs, v_ext, core_density)
    hpsi, ext = pl.pallas_call(
        functools.partial(kernel, (slots, rows_x, rows_y, depth, n_gx, n_yz)),
        out_shape=(pltpu.VMEM(coeffs.shape, BF16), pltpu.VMEM((wide_x, wide_y, depth), F32)),
        in_specs=[hbm, hbm, pl.BlockSpec(memory_space=pltpu.SMEM), hbm, hbm, hbm, hbm],
        out_specs=(vmem, vmem),
        scratch_shapes=[
            pltpu.SMEM(occupation.shape, F32),
            pltpu.SMEM((3, slots), jnp.int32),
            pltpu.VMEM((3, slots), jnp.int32),
            pltpu.VMEM(synthesis.shape, F32),
            pltpu.VMEM(coeffs.shape, BF16),
            pltpu.VMEM(v_ext.shape, F32),
            pltpu.VMEM(v_ext.shape, F32),
            pltpu.VMEM((wide_x, 128), jnp.int32),
            pltpu.SMEM((wide_x, 128), jnp.int32),
            pltpu.VMEM((slots * EDGE, CUBE), BF16),
            pltpu.VMEM((CUBE, CUBE), BF16),
            pltpu.VMEM((CUBE, CUBE), BF16),
            pltpu.VMEM((slots // PAIR, 3 * PAIR * EDGE, PAIR * depth), BF16),
            pltpu.VMEM((slots, CUBE, depth), F32),
            pltpu.VMEM((slots, wide_y * (EDGE + 2) + rows_y, depth), F32),
            pltpu.VMEM((wide_x, wide_y, depth), F32),
            pltpu.VMEM((REACH, wide_y, depth), F32),
            pltpu.VMEM((rows_x, EDGE, depth), F32),
            pltpu.VMEM((slots * EDGE, CUBE), F32),
            pltpu.SemaphoreType.DMA((len(inputs),)),
            pltpu.SemaphoreType.DMA,
            pltpu.SemaphoreType.DMA((exchanges,)),
            pltpu.SemaphoreType.DMA((exchanges,)),
        ],
        compiler_params=pltpu.CompilerParams(
            collective_id=0, has_side_effects=True, vmem_limit_bytes=40 * 1024 * 1024
        ),
    )(*(v if v is live_count else pltpu.with_memory_space_constraint(v, pltpu.HBM) for v in inputs))
    return pl.pallas_call(
        deliver,
        out_shape=(jax.ShapeDtypeStruct(coeffs.shape, BF16), jax.ShapeDtypeStruct(v_ext.shape, F32)),
        in_specs=[vmem, vmem],
        out_specs=(hbm, hbm),
        scratch_shapes=[pltpu.SemaphoreType.DMA((2,))],
        compiler_params=pltpu.CompilerParams(vmem_limit_bytes=16 * 1024 * 1024),
    )(hpsi, ext)


def solution(mesh):
    placed = (
        P(("gx", "yz"), None, None),
        P(("gx", "yz")),
        P(("gx", "yz"), None),
        P(("gx", "yz")),
        P(),
        P("gx", "yz", None),
        P("gx", "yz", None),
    )
    return jax.shard_map(
        functools.partial(shards, mesh.shape["gx"], mesh.shape["yz"]),
        mesh=mesh,
        in_specs=placed,
        out_specs=(P(("gx", "yz"), None, None), P("gx", "yz", None)),
        check_vma=False,
    )
```

time: 33.2 us -> 24.4 us (0.73)
  the two profiles are of different devices: /device:TPU:1 before, /device:TPU:15 now
where the time goes in v2:
time: 24.4 us; the launch traced here: 24.2 us
  Pallas kernels  23 us (94%)
  between operations  1.28 us (5%)
    pallas_call x1, Pallas kernels, shards(): pl.pallas_call(functools.partial(kernel, (slots, rows_x, rows_y, depth, n...  22.1 us
    pallas_call x1, Pallas kernels, shards(): pl.pallas_call(deliver, out_shape=(jax.ShapeDtypeStruct(coeffs.shape, BF1...  0.81 us

profile of v2, /device:TPU:15, one launch (start us, length us, event | category | flops | bytes accessed | tf_op | source)
XLA Modules:
  0.0 24.2 jit_solution(1912494434549750417)
XLA Ops:
  1.3 22.1 %shard_map.86 = (bf16[16,16,256]{2,1,0:T(8,128)(2,1)S(1)}, f32[40,48,128]{2,1,0:T(8,128)S(1)}) custom-call(f32[16]{0:T(128)} %occ_hbm.1, s32[3,16]{1,0:T(4,128)} %bitcast.1, s32[1]{0:T(128)S(6)} %copy.9.live, f32[16,16]{1,0:T(8,128)} %syn_hbm.1, bf16[16,16,256]{2,1,0:T(8,128)(2,1)} %coef_hbm.1, f32[24,32,128]{2,1,0:T(8,128)} %vext_hbm.1, f32[24,32,128]{2,1,0:T(8,128)} %core_hbm.1), custom_call_target="tpu_custom_call" | custom-call | tf_op jit(solution)/shard_map/pallas_call | solution.py:317
  23.4 0.8 %shard_map.87 = (bf16[16,16,256]{2,1,0:T(8,128)(2,1)}, f32[24,32,128]{2,1,0:T(8,128)}) custom-call(bf16[16,16,256]{2,1,0:T(8,128)(2,1)S(1)} %get-tuple-element.4.hpsi_ref, f32[40,48,128]{2,1,0:T(8,128)S(1)} %get-tuple-element.5.ext), custom_call_target="tpu_custom_call" | custom-call | tf_op jit(solution)/shard_map/pallas_call | solution.py:351

commit v3 on v2

--- a/solution.py
+++ b/solution.py
@@ -61,7 +61,7 @@
     occ_hbm, off_hbm, live, syn_hbm, coef_hbm, vext_hbm, core_hbm,
     hpsi_ref, ext,
     occ, off, off_rows, syn_ref, coef, vext, core, start_rows, starts,
-    swapped, kron_hi, kron_lo, filt, psi, padded, partial, from_x, from_y, back,
+    swapped, kron_hi, kron_lo, filt, psi, padded, partial, from_x, from_y, from_after, vext_far, back,
     in_sems, table_sem, send_sems, recv_sems,
 ):
     slots, rows_x, rows_y, depth, n_gx, n_yz = sizes
@@ -98,6 +98,11 @@
     @pl.when(jnp.logical_not(before_y))
     def _():
         from_y[...] = jnp.zeros_like(from_y)
+
+    @pl.when(jnp.logical_not(after_y))
+    def _():
+        from_after[...] = jnp.zeros_like(from_after)
+        vext_far[...] = jnp.zeros_like(vext_far)
 
     def clear(slot, carry):
         for plane in range(EDGE + 3):
@@ -171,9 +176,41 @@
                 padded[f, pl.ds(stride * (a + 1) + rows_y, EDGE), :] = square[a * EDGE : (a + 1) * EDGE, :]
         return carry
 
+    issued = []
+
+    def copy(there, src, dst, device, arrives):
+        index = len(issued)
+        descriptor = pltpu.make_async_remote_copy(
+            src_ref=src, dst_ref=dst, send_sem=send_sems.at[index], recv_sem=recv_sems.at[index],
+            device_id=device, device_id_type=MESH,
+        )
+
+        @pl.when(there)
+        def _():
+            descriptor.start()
+
+        issued.append((there, descriptor))
+
+        def landed():
+            @pl.when(arrives)
+            def _():
+                descriptor.wait_recv()
+
+        return landed
+
+    groups = REACH // GROUP
+    rest = rows_x - REACH
+    edge, inner, far = pl.ds(0, EDGE), pl.ds(EDGE, rows_y - EDGE), pl.ds(rows_y, EDGE)
+    spans = [pl.ds(g * GROUP, GROUP) for g in range(groups)]
+    beyond = [pl.ds(rows_x + g * GROUP, GROUP) for g in range(groups)]
+    others = pl.ds(REACH, rest)
+
+    pl.semaphore_wait(barrier, neighbours)
+    vext_in = copy(before_y, vext_hbm.at[pl.ds(0, REACH), edge], vext_far, last_y, after_y)
+
     lax.fori_loop(0, pairs, synthesize, 0)
 
-    def sum_planes(first, count, unit):
+    def sum_planes(first, count, unit, own):
         def body(step, carry):
             x = first + step * unit
             totals = [None] * unit
@@ -182,87 +219,60 @@
                     rows = padded[f, pl.ds(starts[x + n, f], wide_y), :]
                     totals[n] = rows if f == 0 else totals[n] + rows
             for n in range(unit):
-                partial[x + n] = totals[n]
+                if own:
+                    partial[x + n, :rows_y, :] = totals[n][:rows_y] + core[x + n]
+                    partial[x + n, rows_y:, :] = totals[n][rows_y:]
+                else:
+                    partial[x + n] = totals[n]
             return carry
 
         lax.fori_loop(0, count // unit, body, 0)
 
     table.wait()
-    issued = []
-
-    def copy(there, src, dst, device, arrives):
-        index = len(issued)
-        descriptor = pltpu.make_async_remote_copy(
-            src_ref=src, dst_ref=dst, send_sem=send_sems.at[index], recv_sem=recv_sems.at[index],
-            device_id=device, device_id_type=MESH,
-        )
-
-        @pl.when(there)
-        def _():
-            descriptor.start()
-
-        issued.append((there, descriptor))
-
-        def landed():
-            @pl.when(arrives)
-            def _():
-                descriptor.wait_recv()
-
-        return landed
-
-    groups = REACH // GROUP
-    rest = rows_x - REACH
-    near, far = pl.ds(0, rows_y), pl.ds(rows_y, EDGE)
-    edge, inner = pl.ds(0, EDGE), pl.ds(EDGE, rows_y - EDGE)
-    spans = [pl.ds(g * GROUP, GROUP) for g in range(groups)]
-    beyond = [pl.ds(rows_x + g * GROUP, GROUP) for g in range(groups)]
-    others = pl.ds(REACH, rest)
-
-    corner_in, main_in, side_in = [], [], []
-    for g in range(groups):
-        sum_planes(rows_x + g * GROUP, GROUP, GROUP)
-        if g == 0:
-            pl.semaphore_wait(barrier, neighbours)
-        corner_in.append(copy(after_x, partial.at[beyond[g], far], from_x.at[spans[g], far], next_x, before_x))
-    sum_planes(REACH, rest, 3)
+
+    far_in, edge_in, inner_in = [], [], []
+    for g in range(groups):
+        sum_planes(rows_x + g * GROUP, GROUP, GROUP, False)
+        far_in.append(copy(after_x, partial.at[beyond[g], far], from_x.at[spans[g], far], next_x, before_x))
+        edge_in.append(copy(after_x, partial.at[beyond[g], edge], from_x.at[spans[g], edge], next_x, before_x))
+    load_core.wait()
+    sum_planes(REACH, rest, 3, True)
     rest_in = copy(after_y, partial.at[others, far], from_y.at[others], next_y, before_y)
     for g in range(groups):
-        main_in.append(copy(after_x, partial.at[beyond[g], near], from_x.at[spans[g], near], next_x, before_x))
-    sum_planes(0, REACH, GROUP)
-    for g in range(groups):
-        corner_in[g]()
+        inner_in.append(copy(after_x, partial.at[beyond[g], inner], from_x.at[spans[g], inner], next_x, before_x))
+    sum_planes(0, REACH, GROUP, True)
+
+    onward_in, back_in = [], []
+    for g in range(groups):
+        far_in[g]()
         partial[spans[g], far, :] += from_x[spans[g], far, :]
-        side_in.append(copy(after_y, partial.at[spans[g], far], from_y.at[spans[g]], next_y, before_y))
-
-    def apply(planes, along_x, along_y):
-        rows = edge if along_y else inner
-        density = core[planes, rows, :] + partial[planes, rows, :]
-        if along_x:
-            density = density + from_x[planes, rows, :]
-        if along_y:
-            density = density + from_y[planes]
-        ext[planes, rows, :] = vext[planes, rows, :] + XC_COEF * jnp.exp2(jnp.log2(density) * (1.0 / 3.0))
-
-    load_core.wait()
+        onward_in.append(copy(after_y, partial.at[spans[g], far], from_y.at[spans[g]], next_y, before_y))
+        edge_in[g]()
+        partial[spans[g], edge, :] += from_x[spans[g], edge, :]
+        back_in.append(copy(before_y, partial.at[spans[g], edge], from_after.at[spans[g]], last_y, after_y))
+
+    def potential(planes, rows, external, *densities):
+        density = functools.reduce(jnp.add, densities)
+        ext[planes, rows, :] = external + XC_COEF * jnp.exp2(jnp.log2(density) * (1.0 / 3.0))
+
     load_vext.wait()
+    waits = []
+    for g in range(groups):
+        inner_in[g]()
+        potential(spans[g], inner, vext[spans[g], inner, :], partial[spans[g], inner, :], from_x[spans[g], inner, :])
+        waits.append(copy(before_x, ext.at[spans[g], inner], ext.at[beyond[g], inner], last_x, after_x))
     rest_in()
-    apply(others, False, True)
-    apply(others, False, False)
-    waits = [copy(before_y, ext.at[others, edge], ext.at[others, far], last_y, after_y)]
-    back_in = []
-    for g in range(groups):
-        main_in[g]()
-        apply(spans[g], True, False)
-        waits.append(copy(before_x, ext.at[spans[g], inner], ext.at[beyond[g], inner], last_x, after_x))
-    for g in range(groups):
-        side_in[g]()
-        apply(spans[g], True, True)
-        back_in.append(copy(before_y, ext.at[spans[g], edge], ext.at[spans[g], far], last_y, after_y))
+    potential(others, edge, vext[others, edge, :], partial[others, edge, :], from_y[others])
+    waits.append(copy(before_y, ext.at[others, edge], ext.at[others, far], last_y, after_y))
+    potential(others, inner, vext[others, inner, :], partial[others, inner, :])
+    vext_in()
+    for g in range(groups):
+        onward_in[g]()
+        potential(spans[g], edge, vext[spans[g], edge, :], partial[spans[g], edge, :], from_y[spans[g]])
         waits.append(copy(before_x, ext.at[spans[g], edge], ext.at[beyond[g], edge], last_x, after_x))
-    for g in range(groups):
         back_in[g]()
-        waits.append(copy(
-            before_x & after_y, ext.at[spans[g], far], ext.at[beyond[g], far], last_x, after_x & after_y))
+        potential(spans[g], far, vext_far[spans[g]], partial[spans[g], far, :], from_after[spans[g]])
+        waits.append(copy(before_x, ext.at[spans[g], far], ext.at[beyond[g], far], last_x, after_x))
     for landed in waits:
         landed()
 
@@ -310,7 +320,7 @@
     slots = coeffs.shape[0]
     rows_x, rows_y, depth = v_ext.shape
     wide_x, wide_y = rows_x + EDGE, rows_y + EDGE
-    exchanges = 2 + 7 * (REACH // GROUP)
+    exchanges = 3 + 8 * (REACH // GROUP)
     vmem = pl.BlockSpec(memory_space=pltpu.VMEM)
     hbm = pl.BlockSpec(memory_space=pltpu.HBM)
     inputs = (occupation, box_offset.T, live_count, synthesis, coeffs, v_ext, core_density)
@@ -338,6 +348,8 @@
             pltpu.VMEM((wide_x, wide_y, depth), F32),
             pltpu.VMEM((REACH, wide_y, depth), F32),
             pltpu.VMEM((rows_x, EDGE, depth), F32),
+            pltpu.VMEM((REACH, EDGE, depth), F32),
+            pltpu.VMEM((REACH, EDGE, depth), F32),
             pltpu.VMEM((slots * EDGE, CUBE), F32),
             pltpu.SemaphoreType.DMA((len(inputs),)),
             pltpu.SemaphoreType.DMA,

time: 24.4 us -> 21.9 us (0.90)
  the two profiles are of different devices: /device:TPU:15 before, /device:TPU:97 now
where the time goes in v3:
time: 21.9 us; the launch traced here: 21.8 us
  Pallas kernels  20.5 us (94%)
  between operations  1.28 us (6%)
    pallas_call x1, Pallas kernels, shards(): pl.pallas_call(functools.partial(kernel, (slots, rows_x, rows_y, depth, n...  19.7 us
    pallas_call x1, Pallas kernels, shards(): pl.pallas_call(deliver, out_shape=(jax.ShapeDtypeStruct(coeffs.shape, BF1...  0.81 us

profile of v3, /device:TPU:97, one launch (start us, length us, event | category | flops | bytes accessed | tf_op | source)
XLA Modules:
  0.0 21.8 jit_solution(15855122504852833965)
XLA Ops:
  1.3 19.7 %shard_map.86 = (bf16[16,16,256]{2,1,0:T(8,128)(2,1)S(1)}, f32[40,48,128]{2,1,0:T(8,128)S(1)}) custom-call(f32[16]{0:T(128)} %occ_hbm.1, s32[3,16]{1,0:T(4,128)} %bitcast.1, s32[1]{0:T(128)S(6)} %copy.9.live, f32[16,16]{1,0:T(8,128)} %syn_hbm.1, bf16[16,16,256]{2,1,0:T(8,128)(2,1)} %coef_hbm.1, f32[24,32,128]{2,1,0:T(8,128)} %vext_hbm.1, f32[24,32,128]{2,1,0:T(8,128)} %core_hbm.1), custom_call_target="tpu_custom_call" | custom-call | tf_op jit(solution)/shard_map/pallas_call | solution.py:327
  20.9 0.8 %shard_map.87 = (bf16[16,16,256]{2,1,0:T(8,128)(2,1)}, f32[24,32,128]{2,1,0:T(8,128)}) custom-call(bf16[16,16,256]{2,1,0:T(8,128)(2,1)S(1)} %get-tuple-element.4.hpsi_ref, f32[40,48,128]{2,1,0:T(8,128)S(1)} %get-tuple-element.5.ext), custom_call_target="tpu_custom_call" | custom-call | tf_op jit(solution)/shard_map/pallas_call | solution.py:363

commit v4 on v3

--- a/solution.py
+++ b/solution.py
@@ -61,7 +61,8 @@
     occ_hbm, off_hbm, live, syn_hbm, coef_hbm, vext_hbm, core_hbm,
     hpsi_ref, ext,
     occ, off, off_rows, syn_ref, coef, vext, core, start_rows, starts,
-    swapped, kron_hi, kron_lo, filt, psi, padded, partial, from_x, from_y, from_after, vext_far, back,
+    swapped, kron_hi, kron_lo, filt, psi, padded, partial, from_x, from_y, from_after, vext_far,
+    from_next, vext_next, vext_corner, side_far, side_edge, halo_far, halo_edge, halo_from_y, halo_from_after, back,
     in_sems, table_sem, send_sems, recv_sems,
 ):
     slots, rows_x, rows_y, depth, n_gx, n_yz = sizes
@@ -82,6 +83,9 @@
     after_x, before_x = gx < n_gx - 1, gx > 0
     after_y, before_y = yz < n_yz - 1, yz > 0
     next_x, next_y, last_x, last_y = (gx + 1, yz), (gx, yz + 1), (gx - 1, yz), (gx, yz - 1)
+    odd = lax.rem(gx, 2) == 1
+    even = jnp.logical_not(odd)
+    alone, feeds, takes = odd & after_x, even & before_x, even & after_x
     barrier = pltpu.get_barrier_semaphore()
     neighbours = 0
     for there, device in ((after_x, next_x), (after_y, next_y), (before_x, last_x), (before_y, last_y)):
@@ -98,11 +102,12 @@
     @pl.when(jnp.logical_not(before_y))
     def _():
         from_y[...] = jnp.zeros_like(from_y)
+        halo_from_y[...] = jnp.zeros_like(halo_from_y)
 
     @pl.when(jnp.logical_not(after_y))
     def _():
-        from_after[...] = jnp.zeros_like(from_after)
-        vext_far[...] = jnp.zeros_like(vext_far)
+        for ref in (from_after, halo_from_after, vext_far, vext_corner):
+            ref[...] = jnp.zeros_like(ref)
 
     def clear(slot, carry):
         for plane in range(EDGE + 3):
@@ -206,7 +211,9 @@
     others = pl.ds(REACH, rest)
 
     pl.semaphore_wait(barrier, neighbours)
-    vext_in = copy(before_y, vext_hbm.at[pl.ds(0, REACH), edge], vext_far, last_y, after_y)
+    first = pl.ds(0, REACH)
+    vext_in = copy(before_y, vext_hbm.at[first, edge], vext_far, last_y, after_y)
+    vext_next_in = copy(feeds, vext_hbm.at[first, edge], vext_next, last_x, alone)
 
     lax.fori_loop(0, pairs, synthesize, 0)
 
@@ -230,27 +237,30 @@
 
     table.wait()
 
-    far_in, edge_in, inner_in = [], [], []
+    load_core.wait()
+    sum_planes(REACH, rest, 3, True)
+    rest_in = copy(after_y, partial.at[others, far], from_y.at[others], next_y, before_y)
+    far_in, edge_in, inner_in, next_in = [], [], [], []
     for g in range(groups):
         sum_planes(rows_x + g * GROUP, GROUP, GROUP, False)
         far_in.append(copy(after_x, partial.at[beyond[g], far], from_x.at[spans[g], far], next_x, before_x))
         edge_in.append(copy(after_x, partial.at[beyond[g], edge], from_x.at[spans[g], edge], next_x, before_x))
-    load_core.wait()
-    sum_planes(REACH, rest, 3, True)
-    rest_in = copy(after_y, partial.at[others, far], from_y.at[others], next_y, before_y)
+        sum_planes(g * GROUP, GROUP, GROUP, True)
+        for rows in (far, edge):
+            next_in.append(copy(feeds, partial.at[spans[g], rows], from_next.at[spans[g], rows], last_x, alone))
     for g in range(groups):
         inner_in.append(copy(after_x, partial.at[beyond[g], inner], from_x.at[spans[g], inner], next_x, before_x))
-    sum_planes(0, REACH, GROUP, True)
-
-    onward_in, back_in = [], []
+
+    onward_in, back_in, halo_onward_in, halo_back_in = [], [], [], []
     for g in range(groups):
         far_in[g]()
-        partial[spans[g], far, :] += from_x[spans[g], far, :]
-        onward_in.append(copy(after_y, partial.at[spans[g], far], from_y.at[spans[g]], next_y, before_y))
+        side_far[spans[g]] = partial[spans[g], far, :] + from_x[spans[g], far, :]
+        onward_in.append(copy(after_y, side_far.at[spans[g]], from_y.at[spans[g]], next_y, before_y))
         edge_in[g]()
-        partial[spans[g], edge, :] += from_x[spans[g], edge, :]
-        back_in.append(copy(before_y, partial.at[spans[g], edge], from_after.at[spans[g]], last_y, after_y))
-
+        side_edge[spans[g]] = partial[spans[g], edge, :] + from_x[spans[g], edge, :]
+        back_in.append(copy(before_y, side_edge.at[spans[g]], from_after.at[spans[g]], last_y, after_y))
+    vext_in()
+    vext_corner_in = copy(feeds & after_y, vext_far, vext_corner, last_x, alone & after_y)
     def potential(planes, rows, external, *densities):
         density = functools.reduce(jnp.add, densities)
         ext[planes, rows, :] = external + XC_COEF * jnp.exp2(jnp.log2(density) * (1.0 / 3.0))
@@ -265,14 +275,36 @@
     potential(others, edge, vext[others, edge, :], partial[others, edge, :], from_y[others])
     waits.append(copy(before_y, ext.at[others, edge], ext.at[others, far], last_y, after_y))
     potential(others, inner, vext[others, inner, :], partial[others, inner, :])
-    vext_in()
-    for g in range(groups):
+    for g in range(groups):
+        next_in[2 * g]()
+        next_in[2 * g + 1]()
+
+        @pl.when(alone)
+        def _(g=g):
+            halo_far[spans[g]] = partial[beyond[g], far, :] + from_next[spans[g], far, :]
+            halo_edge[spans[g]] = partial[beyond[g], edge, :] + from_next[spans[g], edge, :]
+
+        halo_onward_in.append(copy(
+            alone & after_y, halo_far.at[spans[g]], halo_from_y.at[spans[g]], next_y, alone & before_y))
+        halo_back_in.append(copy(
+            alone & before_y, halo_edge.at[spans[g]], halo_from_after.at[spans[g]], last_y, alone & after_y))
         onward_in[g]()
-        potential(spans[g], edge, vext[spans[g], edge, :], partial[spans[g], edge, :], from_y[spans[g]])
-        waits.append(copy(before_x, ext.at[spans[g], edge], ext.at[beyond[g], edge], last_x, after_x))
+        potential(spans[g], edge, vext[spans[g], edge, :], side_edge[spans[g]], from_y[spans[g]])
+        waits.append(copy(odd, ext.at[spans[g], edge], ext.at[beyond[g], edge], last_x, takes))
         back_in[g]()
-        potential(spans[g], far, vext_far[spans[g]], partial[spans[g], far, :], from_after[spans[g]])
-        waits.append(copy(before_x, ext.at[spans[g], far], ext.at[beyond[g], far], last_x, after_x))
+        potential(spans[g], far, vext_far[spans[g]], side_far[spans[g]], from_after[spans[g]])
+        waits.append(copy(odd, ext.at[spans[g], far], ext.at[beyond[g], far], last_x, takes))
+    vext_next_in()
+    vext_corner_in()
+    for g in range(groups):
+        halo_onward_in[g]()
+        halo_back_in[g]()
+
+        @pl.when(alone)
+        def _(g=g):
+            potential(beyond[g], edge, vext_next[spans[g]], halo_edge[spans[g]], halo_from_y[spans[g]])
+            potential(beyond[g], far, vext_corner[spans[g]], halo_far[spans[g]], halo_from_after[spans[g]])
+
     for landed in waits:
         landed()
 
@@ -320,7 +352,7 @@
     slots = coeffs.shape[0]
     rows_x, rows_y, depth = v_ext.shape
     wide_x, wide_y = rows_x + EDGE, rows_y + EDGE
-    exchanges = 3 + 8 * (REACH // GROUP)
+    exchanges = 5 + 12 * (REACH // GROUP)
     vmem = pl.BlockSpec(memory_space=pltpu.VMEM)
     hbm = pl.BlockSpec(memory_space=pltpu.HBM)
     inputs = (occupation, box_offset.T, live_count, synthesis, coeffs, v_ext, core_density)
@@ -350,6 +382,8 @@
             pltpu.VMEM((rows_x, EDGE, depth), F32),
             pltpu.VMEM((REACH, EDGE, depth), F32),
             pltpu.VMEM((REACH, EDGE, depth), F32),
+            pltpu.VMEM((REACH, wide_y, depth), F32),
+            *[pltpu.VMEM((REACH, EDGE, depth), F32)] * 8,
             pltpu.VMEM((slots * EDGE, CUBE), F32),
             pltpu.SemaphoreType.DMA((len(inputs),)),
             pltpu.SemaphoreType.DMA,

time: 21.9 us -> 19.7 us (0.90)
  the two profiles are of different devices: /device:TPU:97 before, /device:TPU:1 now
where the time goes in v4:
time: 19.7 us; the launch traced here: 19.6 us
  Pallas kernels  18.3 us (93%)
  between operations  1.28 us (6%)
    pallas_call x1, Pallas kernels, shards(): pl.pallas_call(functools.partial(kernel, (slots, rows_x, rows_y, depth, n...  17.5 us
    pallas_call x1, Pallas kernels, shards(): pl.pallas_call(deliver, out_shape=(jax.ShapeDtypeStruct(coeffs.shape, BF1...  0.81 us

profile of v4, /device:TPU:1, one launch (start us, length us, event | category | flops | bytes accessed | tf_op | source)
XLA Modules:
  0.0 19.6 jit_solution(4822614521810534322)
XLA Ops:
  1.3 17.5 %shard_map.86 = (bf16[16,16,256]{2,1,0:T(8,128)(2,1)S(1)}, f32[40,48,128]{2,1,0:T(8,128)S(1)}) custom-call(f32[16]{0:T(128)} %occ_hbm.1, s32[3,16]{1,0:T(4,128)} %bitcast.1, s32[1]{0:T(128)S(6)} %copy.9.live, f32[16,16]{1,0:T(8,128)} %syn_hbm.1, bf16[16,16,256]{2,1,0:T(8,128)(2,1)} %coef_hbm.1, f32[24,32,128]{2,1,0:T(8,128)} %vext_hbm.1, f32[24,32,128]{2,1,0:T(8,128)} %core_hbm.1), custom_call_target="tpu_custom_call" | custom-call | tf_op jit(solution)/shard_map/pallas_call | solution.py:359
  18.8 0.8 %shard_map.87 = (bf16[16,16,256]{2,1,0:T(8,128)(2,1)}, f32[24,32,128]{2,1,0:T(8,128)}) custom-call(bf16[16,16,256]{2,1,0:T(8,128)(2,1)S(1)} %get-tuple-element.4.hpsi_ref, f32[40,48,128]{2,1,0:T(8,128)S(1)} %get-tuple-element.5.ext), custom_call_target="tpu_custom_call" | custom-call | tf_op jit(solution)/shard_map/pallas_call | solution.py:397

commit v5 on v4

--- a/solution.py
+++ b/solution.py
@@ -11,7 +11,7 @@
 EDGE = 16
 CUBE = EDGE * EDGE
 REACH = EDGE - 1
-PAIR = 4
+CHUNK = 4
 GROUP = 5
 F32 = jnp.float32
 BF16 = jnp.bfloat16
@@ -33,27 +33,29 @@
     return lax.dot_general(left, right, (((1,), (0,)), ((), ())), preferred_element_type=F32)
 
 
-def dot_nt(left, right):
-    return lax.dot_general(left, right, (((1,), (1,)), ((), ())), preferred_element_type=F32)
-
-
-def swap_in_blocks(value):
-    halves = []
-    for half in range(CUBE // 128):
-        part = value[:, half * 128 : (half + 1) * 128].reshape(CUBE // 8, 8, 128)
-        row, col = iota(part.shape, 1), iota(part.shape, 2)
-        for step in (1, 2, 4):
-            up = pltpu.roll(pltpu.roll(part, 8 - step, 1), step, 2)
-            down = pltpu.roll(pltpu.roll(part, step, 1), 128 - step, 2)
-            moved = jnp.where((row & step) != 0, down, up)
-            part = jnp.where(((row ^ col) & step) == 0, part, moved)
-        part = part.reshape(EDGE, 2, 8, 128)
-        first, second = part[:, 0], part[:, 1]
-        far = (iota(first.shape, 2) & 8) != 0
-        new_first = jnp.where(far, pltpu.roll(second, 8, 2), first)
-        new_second = jnp.where(far, second, pltpu.roll(first, 120, 2))
-        halves.append(jnp.stack([new_first, new_second], axis=1).reshape(CUBE, 128))
-    return jnp.concatenate(halves, axis=1)
+def swap_blocks(value):
+    half = EDGE // 2
+    tiles = [
+        [[value[p * EDGE : (p + 1) * EDGE, t * 128 : (t + 1) * 128] for p in range(u * half, (u + 1) * half)] for t in range(2)]
+        for u in range(2)
+    ]
+    block = iota((EDGE, 128), 1) // EDGE
+    rows = []
+    for u in range(2):
+        parts = []
+        for t in range(2):
+            part = tiles[t][u]
+            for step in (1, 2, 4):
+                there = (block & step) != 0
+                part = [
+                    jnp.where(there, part[p], pltpu.roll(part[p - step], 128 - step * EDGE, 1))
+                    if p & step
+                    else jnp.where(there, pltpu.roll(part[p + step], step * EDGE, 1), part[p])
+                    for p in range(half)
+                ]
+            parts.append(jnp.concatenate(part, axis=0))
+        rows.append(jnp.concatenate(parts, axis=1))
+    return jnp.concatenate(rows, axis=0)
 
 
 def kernel(
@@ -61,15 +63,15 @@
     occ_hbm, off_hbm, live, syn_hbm, coef_hbm, vext_hbm, core_hbm,
     hpsi_ref, ext,
     occ, off, off_rows, syn_ref, coef, vext, core, start_rows, starts,
-    swapped, kron_hi, kron_lo, filt, psi, padded, partial, from_x, from_y, from_after, vext_far,
-    from_next, vext_next, vext_corner, side_far, side_edge, halo_far, halo_edge, halo_from_y, halo_from_after, back,
+    kron, back, filt, taps, psi, square, boxes, padded, partial, from_x, from_y, from_after, vext_far,
+    from_next, vext_next, vext_corner, side_far, side_edge, halo_far, halo_edge, halo_from_y, halo_from_after,
     in_sems, table_sem, send_sems, recv_sems,
 ):
     slots, rows_x, rows_y, depth, n_gx, n_yz = sizes
     gx, yz = lax.axis_index("gx"), lax.axis_index("yz")
     wide_y = rows_y + EDGE
     stride = wide_y
-    pairs = slots // PAIR
+    per_half = depth // EDGE
 
     inputs = (
         (coef_hbm, coef), (off_hbm, off), (off_hbm, off_rows), (syn_hbm, syn_ref), (occ_hbm, occ),
@@ -130,55 +132,53 @@
     syn = syn_ref[...]
     lane = iota((EDGE, CUBE), 1)
     row = iota((EDGE, CUBE), 0)
-    by_i = lax.dot(syn, (lane % EDGE == row).astype(F32), precision=HIGHEST, preferred_element_type=F32)
-    by_j = lax.dot(syn, (lane // EDGE == row).astype(F32), precision=HIGHEST, preferred_element_type=F32)
-    for a in range(EDGE):
-        high, low = split(by_i[a : a + 1, :] * by_j)
-        kron_hi[a * EDGE : (a + 1) * EDGE, :] = high
-        kron_lo[a * EDGE : (a + 1) * EDGE, :] = low
-
-    load_off.wait()
-    load_occ.wait()
-    shift = iota((EDGE, depth), 1) - iota((EDGE, depth), 0)
-    places = jnp.concatenate([(shift == off[2, f]).astype(F32) for f in range(slots)], axis=1)
-    placed = lax.dot_general(syn, places, (((0,), (0,)), ((), ())), precision=HIGHEST, preferred_element_type=F32)
-    placed_hi, placed_lo = split(placed)
-    nothing = jnp.zeros((EDGE, depth), BF16)
-    for pair in range(pairs):
-        for piece, source in enumerate((placed_hi, placed_hi, placed_lo)):
-            for h in range(PAIR):
-                f = pair * PAIR + h
-                at = (piece * PAIR + h) * EDGE
-                for lanes in range(PAIR):
-                    what = source[:, f * depth : (f + 1) * depth] if lanes == h else nothing
-                    filt[pair, at : at + EDGE, lanes * depth : (lanes + 1) * depth] = what
+    inside, outside = (lane % EDGE == row).astype(F32), (lane // EDGE == row).astype(F32)
+
+    def exact(contract, right):
+        return lax.dot_general(
+            syn, right, (((contract,), (0,)), ((), ())), precision=HIGHEST, preferred_element_type=F32)
+
+    by_i, by_j, by_a, by_b = exact(1, inside), exact(1, outside), exact(0, outside), exact(0, inside)
+    for n in range(EDGE):
+        rows = slice(n * EDGE, (n + 1) * EDGE)
+        here = lane // EDGE == n
+        for refs, value in (
+            (kron, by_i[n : n + 1, :] * by_j),
+            (back, by_b[n : n + 1, :] * by_a),
+            (filt, jnp.where(here, by_b, 0.0)),
+            (taps, jnp.where(here, by_i, 0.0)),
+        ):
+            high, low = split(value)
+            refs[0, rows, :] = high
+            refs[1, rows, :] = low
 
     def corner(f):
         x = jnp.clip(off[0, f] - gx * rows_x, 0, rows_x - 1)
         y = jnp.clip(off[1, f] - yz * rows_y, 0, rows_y - 1)
         return x, y
 
+    load_off.wait()
+    load_occ.wait()
     load_coef.wait()
-    swapped[...] = swap_in_blocks(coef[...].reshape(slots * EDGE, CUBE).astype(F32)).astype(BF16)
-
-    span = PAIR * EDGE
-
-    def synthesize(pair, carry):
-        part = swapped[pl.ds(pl.multiple_of(pair * span, span), span), :]
-        part = jnp.concatenate([part, part, part], axis=0)
-        inner = dot_nt(kron_hi[...], part) + dot_nt(kron_lo[...], part)
-        high = inner.astype(BF16).astype(F32)
-        where = iota(inner.shape, 1)
-        packed = jnp.where((where >= span) & (where < 2 * span), inner - high, high).astype(BF16)
-        values = dot(packed, filt[pair])
-        for h in range(PAIR):
-            f = pair * PAIR + h
-            value = values[:, h * depth : (h + 1) * depth]
-            psi[f] = value
-            weight = jnp.where(f < live[0], occ[f], 0.0)
-            square = value * value * weight
+    swapped = swap_blocks(coef[...].reshape(slots * EDGE, CUBE).astype(F32)).astype(BF16)
+    inner_high, inner_low = split(dot(kron[0], swapped) + dot(kron[1], swapped))
+    psi[...] = dot(inner_high, filt[0]) + (dot(inner_low, filt[0]) + dot(inner_high, filt[1]))
+
+    owner = iota((1, CUBE), 1) // EDGE
+    weights = jnp.zeros((1, CUBE), F32)
+    for f in range(slots):
+        weights = jnp.where(owner == f, jnp.where(f < live[0], occ[f], 0.0), weights)
+    square[...] = psi[...] * psi[...] * weights
+
+    def place(n, carry):
+        for half in range(CUBE // depth):
+            f = half * per_half + n
+            z = off[2, f]
+            value = pltpu.roll(square[:, half * depth : (half + 1) * depth], lax.rem(z - n * EDGE + depth, depth), 1)
+            along = iota((1, depth), 1) - z
+            value = jnp.where((along >= 0) & (along < EDGE), value, 0.0)
             for a in range(EDGE):
-                padded[f, pl.ds(stride * (a + 1) + rows_y, EDGE), :] = square[a * EDGE : (a + 1) * EDGE, :]
+                padded[f, pl.ds(stride * (a + 1) + rows_y, EDGE), :] = value[a * EDGE : (a + 1) * EDGE, :]
         return carry
 
     issued = []
@@ -215,7 +215,7 @@
     vext_in = copy(before_y, vext_hbm.at[first, edge], vext_far, last_y, after_y)
     vext_next_in = copy(feeds, vext_hbm.at[first, edge], vext_next, last_x, alone)
 
-    lax.fori_loop(0, pairs, synthesize, 0)
+    lax.fori_loop(0, per_half, place, 0)
 
     def sum_planes(first, count, unit, own):
         def body(step, carry):
@@ -308,24 +308,25 @@
     for landed in waits:
         landed()
 
-    def analyze(pair, carry):
-        parts = []
-        for h in range(PAIR):
-            f = pair * PAIR + h
-            x, y = corner(f)
-            box = ext[pl.ds(x, EDGE), pl.ds(y, EDGE), :].reshape(CUBE, depth)
-            parts.append(box * psi[f])
-        high, low = split(jnp.concatenate(parts, axis=1))
-        left = filt[pair]
-        both = dot_nt(left[span:], high)
-        inner = both[:span] + both[span:] + dot_nt(left[:span], low)
-        back[pl.ds(pl.multiple_of(pair * span, span), span), :] = inner
+    def collect(part, carry):
+        rows = pl.ds(pl.multiple_of(part * CHUNK * EDGE, CHUNK * EDGE), CHUNK * EDGE)
+        block = iota((1, depth), 1) // EDGE
+        for half in range(CUBE // depth):
+            total = None
+            for n in range(per_half):
+                f = half * per_half + n
+                x, y = corner(f)
+                box = ext[pl.ds(x + part * CHUNK, CHUNK), pl.ds(y, EDGE), :].reshape(CHUNK * EDGE, depth)
+                box = pltpu.roll(box, lax.rem(n * EDGE - off[2, f] + depth, depth), 1)
+                total = box if n == 0 else jnp.where(block == n, box, total)
+            boxes[rows, half * depth : (half + 1) * depth] = total
         return carry
 
-    lax.fori_loop(0, pairs, analyze, 0)
-    high, low = split(back[...])
-    result = dot(high, kron_hi[...]) + (dot(high, kron_lo[...]) + dot(low, kron_hi[...]))
-    result = swap_in_blocks(result)
+    lax.fori_loop(0, EDGE // CHUNK, collect, 0)
+    high, low = split(boxes[...] * psi[...])
+    high, low = split(dot(high, taps[0]) + (dot(high, taps[1]) + dot(low, taps[0])))
+    result = dot(back[0], high) + (dot(back[0], low) + dot(back[1], high))
+    result = swap_blocks(result)
     used = iota(result.shape, 0) < live[0] * EDGE
     result = jnp.where(used, result, 0.0)
     hpsi_ref[...] = result.astype(BF16).reshape(slots, EDGE, CUBE)
@@ -371,11 +372,8 @@
             pltpu.VMEM(v_ext.shape, F32),
             pltpu.VMEM((wide_x, 128), jnp.int32),
             pltpu.SMEM((wide_x, 128), jnp.int32),
-            pltpu.VMEM((slots * EDGE, CUBE), BF16),
-            pltpu.VMEM((CUBE, CUBE), BF16),
-            pltpu.VMEM((CUBE, CUBE), BF16),
-            pltpu.VMEM((slots // PAIR, 3 * PAIR * EDGE, PAIR * depth), BF16),
-            pltpu.VMEM((slots, CUBE, depth), F32),
+            *[pltpu.VMEM((2, CUBE, CUBE), BF16)] * 4,
+            *[pltpu.VMEM((CUBE, CUBE), F32)] * 3,
             pltpu.VMEM((slots, wide_y * (EDGE + 2) + rows_y, depth), F32),
             pltpu.VMEM((wide_x, wide_y, depth), F32),
             pltpu.VMEM((REACH, wide_y, depth), F32),
@@ -384,7 +382,6 @@
             pltpu.VMEM((REACH, EDGE, depth), F32),
             pltpu.VMEM((REACH, wide_y, depth), F32),
             *[pltpu.VMEM((REACH, EDGE, depth), F32)] * 8,
-            pltpu.VMEM((slots * EDGE, CUBE), F32),
             pltpu.SemaphoreType.DMA((len(inputs),)),
             pltpu.SemaphoreType.DMA,
             pltpu.SemaphoreType.DMA((exchanges,)),

time: 19.7 us -> 18.8 us (0.954)
  Pallas kernels: 18.3 us -> 17.4 us
    pallas_call x1, Pallas kernels: 17.5 us -> 16.5 us  [shards(): pl.pallas_call(functools.partial(kernel, (slots, rows_x, rows_y, depth, n...]
where the time goes in v5:
time: 18.8 us; the launch traced here: 18.6 us
  Pallas kernels  17.4 us (93%)
  between operations  1.28 us (7%)
    pallas_call x1, Pallas kernels, shards(): pl.pallas_call(functools.partial(kernel, (slots, rows_x, rows_y, depth, n...  16.5 us
    pallas_call x1, Pallas kernels, shards(): pl.pallas_call(deliver, out_shape=(jax.ShapeDtypeStruct(coeffs.shape, BF1...  0.81 us

profile of v5, /device:TPU:1, one launch (start us, length us, event | category | flops | bytes accessed | tf_op | source)
XLA Modules:
  0.0 18.6 jit_solution(2304418291473150358)
XLA Ops:
  1.3 16.5 %shard_map.86 = (bf16[16,16,256]{2,1,0:T(8,128)(2,1)S(1)}, f32[40,48,128]{2,1,0:T(8,128)S(1)}) custom-call(f32[16]{0:T(128)} %occ_hbm.1, s32[3,16]{1,0:T(4,128)} %bitcast.1, s32[1]{0:T(128)S(6)} %copy.9.live, f32[16,16]{1,0:T(8,128)} %syn_hbm.1, bf16[16,16,256]{2,1,0:T(8,128)(2,1)} %coef_hbm.1, f32[24,32,128]{2,1,0:T(8,128)} %vext_hbm.1, f32[24,32,128]{2,1,0:T(8,128)} %core_hbm.1), custom_call_target="tpu_custom_call" | custom-call | tf_op jit(solution)/shard_map/pallas_call | solution.py:360
  17.8 0.8 %shard_map.87 = (bf16[16,16,256]{2,1,0:T(8,128)(2,1)}, f32[24,32,128]{2,1,0:T(8,128)}) custom-call(bf16[16,16,256]{2,1,0:T(8,128)(2,1)S(1)} %get-tuple-element.4.hpsi_ref, f32[40,48,128]{2,1,0:T(8,128)S(1)} %get-tuple-element.5.ext), custom_call_target="tpu_custom_call" | custom-call | tf_op jit(solution)/shard_map/pallas_call | solution.py:394

commit v6 on v5

--- a/solution.py
+++ b/solution.py
@@ -61,9 +61,9 @@
 def kernel(
     sizes,
     occ_hbm, off_hbm, live, syn_hbm, coef_hbm, vext_hbm, core_hbm,
-    hpsi_ref, ext,
-    occ, off, off_rows, syn_ref, coef, vext, core, start_rows, starts,
-    kron, back, filt, taps, psi, square, boxes, padded, partial, from_x, from_y, from_after, vext_far,
+    boxes, back, ext,
+    occ, off_rows, syn_ref, coef, vext, core, start_rows, starts,
+    kron, filt, taps, psi, square, padded, partial, from_x, from_y, from_after, vext_far,
     from_next, vext_next, vext_corner, side_far, side_edge, halo_far, halo_edge, halo_from_y, halo_from_after,
     in_sems, table_sem, send_sems, recv_sems,
 ):
@@ -74,13 +74,13 @@
     per_half = depth // EDGE
 
     inputs = (
-        (coef_hbm, coef), (off_hbm, off), (off_hbm, off_rows), (syn_hbm, syn_ref), (occ_hbm, occ),
+        (coef_hbm, coef), (off_hbm, off_rows), (syn_hbm, syn_ref), (occ_hbm, occ),
         (core_hbm, core), (vext_hbm, vext),
     )
     loads = [pltpu.make_async_copy(src, dst, in_sems.at[n]) for n, (src, dst) in enumerate(inputs)]
     for load in loads:
         load.start()
-    load_coef, load_off, load_off_rows, load_syn, load_occ, load_core, load_vext = loads
+    load_coef, load_off_rows, load_syn, load_occ, load_core, load_vext = loads
 
     after_x, before_x = gx < n_gx - 1, gx > 0
     after_y, before_y = yz < n_yz - 1, yz > 0
@@ -120,11 +120,16 @@
 
     lax.fori_loop(0, slots, clear, 0)
 
+    at_x, at_y, at_z, turn_to, turn_from = (rows_x + EDGE + n for n in range(5))
     load_off_rows.wait()
     begin_x = jnp.clip(off_rows[0:1, :] - gx * rows_x, 0, rows_x - 1)
     begin_y = jnp.clip(off_rows[1:2, :] - yz * rows_y, 0, rows_y - 1)
     plane = jnp.clip(iota((rows_x + EDGE, slots), 0) - begin_x + 1, 0, EDGE + 1)
-    start_rows[:, :slots] = plane * stride + rows_y - begin_y
+    begin_z = off_rows[2:3, :]
+    turn = begin_z - (iota((1, slots), 1) % per_half) * EDGE
+    start_rows[: rows_x + EDGE, :slots] = plane * stride + rows_y - begin_y
+    for n, value in enumerate((begin_x, begin_y, begin_z, turn & (depth - 1), (-turn) & (depth - 1))):
+        start_rows[rows_x + EDGE + n : rows_x + EDGE + n + 1, :slots] = value
     table = pltpu.make_async_copy(start_rows, starts, table_sem)
     table.start()
 
@@ -152,12 +157,6 @@
             refs[0, rows, :] = high
             refs[1, rows, :] = low
 
-    def corner(f):
-        x = jnp.clip(off[0, f] - gx * rows_x, 0, rows_x - 1)
-        y = jnp.clip(off[1, f] - yz * rows_y, 0, rows_y - 1)
-        return x, y
-
-    load_off.wait()
     load_occ.wait()
     load_coef.wait()
     swapped = swap_blocks(coef[...].reshape(slots * EDGE, CUBE).astype(F32)).astype(BF16)
@@ -173,9 +172,8 @@
     def place(n, carry):
         for half in range(CUBE // depth):
             f = half * per_half + n
-            z = off[2, f]
-            value = pltpu.roll(square[:, half * depth : (half + 1) * depth], lax.rem(z - n * EDGE + depth, depth), 1)
-            along = iota((1, depth), 1) - z
+            value = pltpu.roll(square[:, half * depth : (half + 1) * depth], starts[turn_to, f], 1)
+            along = iota((1, depth), 1) - starts[at_z, f]
             value = jnp.where((along >= 0) & (along < EDGE), value, 0.0)
             for a in range(EDGE):
                 padded[f, pl.ds(stride * (a + 1) + rows_y, EDGE), :] = value[a * EDGE : (a + 1) * EDGE, :]
@@ -213,9 +211,9 @@
     pl.semaphore_wait(barrier, neighbours)
     first = pl.ds(0, REACH)
     vext_in = copy(before_y, vext_hbm.at[first, edge], vext_far, last_y, after_y)
-    vext_next_in = copy(feeds, vext_hbm.at[first, edge], vext_next, last_x, alone)
-
-    lax.fori_loop(0, per_half, place, 0)
+
+    table.wait()
+    lax.fori_loop(0, per_half, place, 0, unroll=2)
 
     def sum_planes(first, count, unit, own):
         def body(step, carry):
@@ -235,8 +233,6 @@
 
         lax.fori_loop(0, count // unit, body, 0)
 
-    table.wait()
-
     load_core.wait()
     sum_planes(REACH, rest, 3, True)
     rest_in = copy(after_y, partial.at[others, far], from_y.at[others], next_y, before_y)
@@ -248,6 +244,7 @@
         sum_planes(g * GROUP, GROUP, GROUP, True)
         for rows in (far, edge):
             next_in.append(copy(feeds, partial.at[spans[g], rows], from_next.at[spans[g], rows], last_x, alone))
+    vext_next_in = copy(feeds, vext_hbm.at[first, edge], vext_next, last_x, alone)
     for g in range(groups):
         inner_in.append(copy(after_x, partial.at[beyond[g], inner], from_x.at[spans[g], inner], next_x, before_x))
 
@@ -267,13 +264,13 @@
 
     load_vext.wait()
     waits = []
+    rest_in()
+    potential(others, edge, vext[others, edge, :], partial[others, edge, :], from_y[others])
+    waits.append(copy(before_y, ext.at[others, edge], ext.at[others, far], last_y, after_y))
     for g in range(groups):
         inner_in[g]()
         potential(spans[g], inner, vext[spans[g], inner, :], partial[spans[g], inner, :], from_x[spans[g], inner, :])
         waits.append(copy(before_x, ext.at[spans[g], inner], ext.at[beyond[g], inner], last_x, after_x))
-    rest_in()
-    potential(others, edge, vext[others, edge, :], partial[others, edge, :], from_y[others])
-    waits.append(copy(before_y, ext.at[others, edge], ext.at[others, far], last_y, after_y))
     potential(others, inner, vext[others, inner, :], partial[others, inner, :])
     for g in range(groups):
         next_in[2 * g]()
@@ -311,42 +308,41 @@
     def collect(part, carry):
         rows = pl.ds(pl.multiple_of(part * CHUNK * EDGE, CHUNK * EDGE), CHUNK * EDGE)
         block = iota((1, depth), 1) // EDGE
+        totals = []
         for half in range(CUBE // depth):
             total = None
             for n in range(per_half):
                 f = half * per_half + n
-                x, y = corner(f)
-                box = ext[pl.ds(x + part * CHUNK, CHUNK), pl.ds(y, EDGE), :].reshape(CHUNK * EDGE, depth)
-                box = pltpu.roll(box, lax.rem(n * EDGE - off[2, f] + depth, depth), 1)
+                box = ext[pl.ds(starts[at_x, f] + part * CHUNK, CHUNK), pl.ds(starts[at_y, f], EDGE), :]
+                box = pltpu.roll(box.reshape(CHUNK * EDGE, depth), starts[turn_from, f], 1)
                 total = box if n == 0 else jnp.where(block == n, box, total)
-            boxes[rows, half * depth : (half + 1) * depth] = total
+            totals.append(total)
+        high, low = split(jnp.concatenate(totals, axis=1) * psi[rows, :])
+        value = dot(high, taps[0]) + (dot(high, taps[1]) + dot(low, taps[0]))
+        high, low = split(jnp.where(iota((1, CUBE), 1) < live[0] * EDGE, value, 0.0))
+        boxes[0, rows, :] = high
+        boxes[1, rows, :] = low
         return carry
 
-    lax.fori_loop(0, EDGE // CHUNK, collect, 0)
-    high, low = split(boxes[...] * psi[...])
-    high, low = split(dot(high, taps[0]) + (dot(high, taps[1]) + dot(low, taps[0])))
-    result = dot(back[0], high) + (dot(back[0], low) + dot(back[1], high))
-    result = swap_blocks(result)
-    used = iota(result.shape, 0) < live[0] * EDGE
-    result = jnp.where(used, result, 0.0)
-    hpsi_ref[...] = result.astype(BF16).reshape(slots, EDGE, CUBE)
-
+    lax.fori_loop(0, EDGE // CHUNK, collect, 0, unroll=4)
     for there, descriptor in issued:
         @pl.when(there)
         def _(descriptor=descriptor):
             descriptor.wait_send()
 
 
-def deliver(hpsi_ref, ext, hpsi_hbm, pot_hbm, sems):
+def deliver(boxes, back, ext, hpsi_hbm, pot_hbm, hpsi, sems):
+    slots, _, _ = hpsi_hbm.shape
     rows_x, rows_y, _ = pot_hbm.shape
-    copies = (
-        pltpu.make_async_copy(hpsi_ref, hpsi_hbm, sems.at[0]),
-        pltpu.make_async_copy(ext.at[pl.ds(0, rows_x), pl.ds(0, rows_y)], pot_hbm, sems.at[1]),
-    )
-    for copy in copies:
-        copy.start()
-    for copy in copies:
-        copy.wait()
+    pot_out = pltpu.make_async_copy(ext.at[pl.ds(0, rows_x), pl.ds(0, rows_y)], pot_hbm, sems.at[0])
+    pot_out.start()
+    high, low = boxes[0], boxes[1]
+    result = dot(back[0], high) + (dot(back[0], low) + dot(back[1], high))
+    hpsi[...] = swap_blocks(result).astype(BF16).reshape(slots, EDGE, CUBE)
+    hpsi_out = pltpu.make_async_copy(hpsi, hpsi_hbm, sems.at[1])
+    hpsi_out.start()
+    pot_out.wait()
+    hpsi_out.wait()
 
 
 def shards(n_gx, n_yz, coeffs, occupation, box_offset, live_count, synthesis, v_ext, core_density):
@@ -357,23 +353,26 @@
     vmem = pl.BlockSpec(memory_space=pltpu.VMEM)
     hbm = pl.BlockSpec(memory_space=pltpu.HBM)
     inputs = (occupation, box_offset.T, live_count, synthesis, coeffs, v_ext, core_density)
-    hpsi, ext = pl.pallas_call(
+    boxes, back, ext = pl.pallas_call(
         functools.partial(kernel, (slots, rows_x, rows_y, depth, n_gx, n_yz)),
-        out_shape=(pltpu.VMEM(coeffs.shape, BF16), pltpu.VMEM((wide_x, wide_y, depth), F32)),
+        out_shape=(
+            pltpu.VMEM((2, CUBE, CUBE), BF16),
+            pltpu.VMEM((2, CUBE, CUBE), BF16),
+            pltpu.VMEM((wide_x, wide_y, depth), F32),
+        ),
         in_specs=[hbm, hbm, pl.BlockSpec(memory_space=pltpu.SMEM), hbm, hbm, hbm, hbm],
-        out_specs=(vmem, vmem),
+        out_specs=(vmem, vmem, vmem),
         scratch_shapes=[
             pltpu.SMEM(occupation.shape, F32),
-            pltpu.SMEM((3, slots), jnp.int32),
             pltpu.VMEM((3, slots), jnp.int32),
             pltpu.VMEM(synthesis.shape, F32),
             pltpu.VMEM(coeffs.shape, BF16),
             pltpu.VMEM(v_ext.shape, F32),
             pltpu.VMEM(v_ext.shape, F32),
-            pltpu.VMEM((wide_x, 128), jnp.int32),
-            pltpu.SMEM((wide_x, 128), jnp.int32),
-            *[pltpu.VMEM((2, CUBE, CUBE), BF16)] * 4,
-            *[pltpu.VMEM((CUBE, CUBE), F32)] * 3,
+            pltpu.VMEM((wide_x + 8, 128), jnp.int32),
+            pltpu.SMEM((wide_x + 8, 128), jnp.int32),
+            *[pltpu.VMEM((2, CUBE, CUBE), BF16)] * 3,
+            *[pltpu.VMEM((CUBE, CUBE), F32)] * 2,
             pltpu.VMEM((slots, wide_y * (EDGE + 2) + rows_y, depth), F32),
             pltpu.VMEM((wide_x, wide_y, depth), F32),
             pltpu.VMEM((REACH, wide_y, depth), F32),
@@ -382,7 +381,7 @@
             pltpu.VMEM((REACH, EDGE, depth), F32),
             pltpu.VMEM((REACH, wide_y, depth), F32),
             *[pltpu.VMEM((REACH, EDGE, depth), F32)] * 8,
-            pltpu.SemaphoreType.DMA((len(inputs),)),
+            pltpu.SemaphoreType.DMA((len(inputs) - 1,)),
             pltpu.SemaphoreType.DMA,
             pltpu.SemaphoreType.DMA((exchanges,)),
             pltpu.SemaphoreType.DMA((exchanges,)),
@@ -394,11 +393,11 @@
     return pl.pallas_call(
         deliver,
         out_shape=(jax.ShapeDtypeStruct(coeffs.shape, BF16), jax.ShapeDtypeStruct(v_ext.shape, F32)),
-        in_specs=[vmem, vmem],
+        in_specs=[vmem, vmem, vmem],
         out_specs=(hbm, hbm),
-        scratch_shapes=[pltpu.SemaphoreType.DMA((2,))],
+        scratch_shapes=[pltpu.VMEM(coeffs.shape, BF16), pltpu.SemaphoreType.DMA((2,))],
         compiler_params=pltpu.CompilerParams(vmem_limit_bytes=16 * 1024 * 1024),
-    )(hpsi, ext)
+    )(boxes, back, ext)
 
 
 def solution(mesh):

time: 18.8 us -> 18.3 us (0.973)
  Pallas kernels: 17.4 us -> 16.8 us
    pallas_call x1, Pallas kernels: 16.5 us -> 15.7 us  [shards(): pl.pallas_call(functools.partial(kernel, (slots, rows_x, rows_y, depth, n...]
    pallas_call x1, Pallas kernels: 0.81 us -> 1.17 us  [shards(): pl.pallas_call(deliver, out_shape=(jax.ShapeDtypeStruct(coeffs.shape, BF1...]
where the time goes in v6:
time: 18.3 us; the launch traced here: 18.1 us
  Pallas kernels  16.8 us (92%)
  between operations  1.29 us (7%)
    pallas_call x1, Pallas kernels, shards(): pl.pallas_call(functools.partial(kernel, (slots, rows_x, rows_y, depth, n...  15.7 us
    pallas_call x1, Pallas kernels, shards(): pl.pallas_call(deliver, out_shape=(jax.ShapeDtypeStruct(coeffs.shape, BF1...  1.17 us

profile of v6, /device:TPU:1, one launch (start us, length us, event | category | flops | bytes accessed | tf_op | source)
XLA Modules:
  0.0 18.1 jit_solution(14508286848949824782)
XLA Ops:
  1.3 15.7 %shard_map.86 = (bf16[2,256,256]{2,1,0:T(8,128)(2,1)S(1)}, bf16[2,256,256]{2,1,0:T(8,128)(2,1)S(1)}, f32[40,48,128]{2,1,0:T(8,128)S(1)}) custom-call(f32[16]{0:T(128)} %occ_hbm.1, s32[3,16]{1,0:T(4,128)} %bitcast.1, s32[1]{0:T(128)S(6)} %copy.9.live, f32[16,16]{1,0:T(8,128)} %syn_hbm.1, bf16[16,16,256]{2,1,0:T(8,128)(2,1)} %coef_hbm.1, ...), custom_call_target="tpu_custom_call" | custom-call | tf_op jit(solution)/shard_map/pallas_call | solution.py:356
  17.0 1.2 %shard_map.87 = (bf16[16,16,256]{2,1,0:T(8,128)(2,1)}, f32[24,32,128]{2,1,0:T(8,128)}) custom-call(bf16[2,256,256]{2,1,0:T(8,128)(2,1)S(1)} %get-tuple-element.5.boxes, bf16[2,256,256]{2,1,0:T(8,128)(2,1)S(1)} %get-tuple-element.6.back, f32[40,48,128]{2,1,0:T(8,128)S(1)} %get-tuple-element.7.ext), custom_call_target="tpu_custom_call" | custom-call | tf_op jit(solution)/shard_map/pallas_call | solution.py:393

commit v7 on v6

--- a/solution.py
+++ b/solution.py
@@ -97,6 +97,9 @@
 
         neighbours = neighbours + there.astype(jnp.int32)
 
+    for ref in (from_y, halo_from_y):
+        ref[:, REACH:, :] = jnp.zeros((ref.shape[0], EDGE - REACH, depth), F32)
+
     @pl.when(jnp.logical_not(before_x))
     def _():
         from_x[...] = jnp.zeros_like(from_x)
@@ -204,13 +207,15 @@
     groups = REACH // GROUP
     rest = rows_x - REACH
     edge, inner, far = pl.ds(0, EDGE), pl.ds(EDGE, rows_y - EDGE), pl.ds(rows_y, EDGE)
+    edge_sent, far_sent = pl.ds(0, REACH), pl.ds(rows_y, REACH)
     spans = [pl.ds(g * GROUP, GROUP) for g in range(groups)]
     beyond = [pl.ds(rows_x + g * GROUP, GROUP) for g in range(groups)]
     others = pl.ds(REACH, rest)
 
     pl.semaphore_wait(barrier, neighbours)
+    load_vext.wait()
     first = pl.ds(0, REACH)
-    vext_in = copy(before_y, vext_hbm.at[first, edge], vext_far, last_y, after_y)
+    vext_in = copy(before_y, vext.at[first, edge_sent], vext_far.at[:, edge_sent], last_y, after_y)
 
     table.wait()
     lax.fori_loop(0, per_half, place, 0, unroll=2)
@@ -235,38 +240,37 @@
 
     load_core.wait()
     sum_planes(REACH, rest, 3, True)
-    rest_in = copy(after_y, partial.at[others, far], from_y.at[others], next_y, before_y)
+    rest_in = copy(after_y, partial.at[others, far_sent], from_y.at[others, edge_sent], next_y, before_y)
     far_in, edge_in, inner_in, next_in = [], [], [], []
     for g in range(groups):
         sum_planes(rows_x + g * GROUP, GROUP, GROUP, False)
-        far_in.append(copy(after_x, partial.at[beyond[g], far], from_x.at[spans[g], far], next_x, before_x))
+        far_in.append(copy(after_x, partial.at[beyond[g], far_sent], from_x.at[spans[g], far_sent], next_x, before_x))
         edge_in.append(copy(after_x, partial.at[beyond[g], edge], from_x.at[spans[g], edge], next_x, before_x))
         sum_planes(g * GROUP, GROUP, GROUP, True)
-        for rows in (far, edge):
+        for rows in (far_sent, edge):
             next_in.append(copy(feeds, partial.at[spans[g], rows], from_next.at[spans[g], rows], last_x, alone))
-    vext_next_in = copy(feeds, vext_hbm.at[first, edge], vext_next, last_x, alone)
-    for g in range(groups):
-        inner_in.append(copy(after_x, partial.at[beyond[g], inner], from_x.at[spans[g], inner], next_x, before_x))
+    vext_next_in = copy(feeds, vext.at[first, edge], vext_next, last_x, alone)
 
     onward_in, back_in, halo_onward_in, halo_back_in = [], [], [], []
     for g in range(groups):
         far_in[g]()
         side_far[spans[g]] = partial[spans[g], far, :] + from_x[spans[g], far, :]
-        onward_in.append(copy(after_y, side_far.at[spans[g]], from_y.at[spans[g]], next_y, before_y))
+        onward_in.append(copy(after_y, side_far.at[spans[g], edge_sent], from_y.at[spans[g], edge_sent], next_y, before_y))
         edge_in[g]()
         side_edge[spans[g]] = partial[spans[g], edge, :] + from_x[spans[g], edge, :]
-        back_in.append(copy(before_y, side_edge.at[spans[g]], from_after.at[spans[g]], last_y, after_y))
+        back_in.append(copy(before_y, side_edge.at[spans[g], edge_sent], from_after.at[spans[g], edge_sent], last_y, after_y))
+    for g in range(groups):
+        inner_in.append(copy(after_x, partial.at[beyond[g], inner], from_x.at[spans[g], inner], next_x, before_x))
     vext_in()
-    vext_corner_in = copy(feeds & after_y, vext_far, vext_corner, last_x, alone & after_y)
+    vext_corner_in = copy(feeds & after_y, vext_far.at[:, edge_sent], vext_corner.at[:, edge_sent], last_x, alone & after_y)
     def potential(planes, rows, external, *densities):
         density = functools.reduce(jnp.add, densities)
         ext[planes, rows, :] = external + XC_COEF * jnp.exp2(jnp.log2(density) * (1.0 / 3.0))
 
-    load_vext.wait()
     waits = []
     rest_in()
     potential(others, edge, vext[others, edge, :], partial[others, edge, :], from_y[others])
-    waits.append(copy(before_y, ext.at[others, edge], ext.at[others, far], last_y, after_y))
+    waits.append(copy(before_y, ext.at[others, edge_sent], ext.at[others, far_sent], last_y, after_y))
     for g in range(groups):
         inner_in[g]()
         potential(spans[g], inner, vext[spans[g], inner, :], partial[spans[g], inner, :], from_x[spans[g], inner, :])
@@ -282,15 +286,15 @@
             halo_edge[spans[g]] = partial[beyond[g], edge, :] + from_next[spans[g], edge, :]
 
         halo_onward_in.append(copy(
-            alone & after_y, halo_far.at[spans[g]], halo_from_y.at[spans[g]], next_y, alone & before_y))
+            alone & after_y, halo_far.at[spans[g], edge_sent], halo_from_y.at[spans[g], edge_sent], next_y, alone & before_y))
         halo_back_in.append(copy(
-            alone & before_y, halo_edge.at[spans[g]], halo_from_after.at[spans[g]], last_y, alone & after_y))
+            alone & before_y, halo_edge.at[spans[g], edge_sent], halo_from_after.at[spans[g], edge_sent], last_y, alone & after_y))
         onward_in[g]()
         potential(spans[g], edge, vext[spans[g], edge, :], side_edge[spans[g]], from_y[spans[g]])
         waits.append(copy(odd, ext.at[spans[g], edge], ext.at[beyond[g], edge], last_x, takes))
         back_in[g]()
         potential(spans[g], far, vext_far[spans[g]], side_far[spans[g]], from_after[spans[g]])
-        waits.append(copy(odd, ext.at[spans[g], far], ext.at[beyond[g], far], last_x, takes))
+        waits.append(copy(odd, ext.at[spans[g], far_sent], ext.at[beyond[g], far_sent], last_x, takes))
     vext_next_in()
     vext_corner_in()
     for g in range(groups):

time: 18.3 us -> 18.1 us (0.989)
  no operation moved by 1% of the time
where the time goes in v7:
time: 18.1 us; the launch traced here: 18 us
  Pallas kernels  16.7 us (92%)
  between operations  1.29 us (7%)
    pallas_call x1, Pallas kernels, shards(): pl.pallas_call(functools.partial(kernel, (slots, rows_x, rows_y, depth, n...  15.5 us
    pallas_call x1, Pallas kernels, shards(): pl.pallas_call(deliver, out_shape=(jax.ShapeDtypeStruct(coeffs.shape, BF1...  1.16 us

profile of v7, /device:TPU:1, one launch (start us, length us, event | category | flops | bytes accessed | tf_op | source)
XLA Modules:
  0.0 18.0 jit_solution(7348584685836445653)
XLA Ops:
  1.3 15.5 %shard_map.86 = (bf16[2,256,256]{2,1,0:T(8,128)(2,1)S(1)}, bf16[2,256,256]{2,1,0:T(8,128)(2,1)S(1)}, f32[40,48,128]{2,1,0:T(8,128)S(1)}) custom-call(f32[16]{0:T(128)} %occ_hbm.1, s32[3,16]{1,0:T(4,128)} %bitcast.1, s32[1]{0:T(128)S(6)} %copy.9.live, f32[16,16]{1,0:T(8,128)} %syn_hbm.1, bf16[16,16,256]{2,1,0:T(8,128)(2,1)} %coef_hbm.1, ...), custom_call_target="tpu_custom_call" | custom-call | tf_op jit(solution)/shard_map/pallas_call | solution.py:360
  16.8 1.2 %shard_map.87 = (bf16[16,16,256]{2,1,0:T(8,128)(2,1)}, f32[24,32,128]{2,1,0:T(8,128)}) custom-call(bf16[2,256,256]{2,1,0:T(8,128)(2,1)S(1)} %get-tuple-element.5.boxes, bf16[2,256,256]{2,1,0:T(8,128)(2,1)S(1)} %get-tuple-element.6.back, f32[40,48,128]{2,1,0:T(8,128)S(1)} %get-tuple-element.7.ext), custom_call_target="tpu_custom_call" | custom-call | tf_op jit(solution)/shard_map/pallas_call | solution.py:397

commit v8 on v7

--- a/solution.py
+++ b/solution.py
@@ -218,7 +218,7 @@
     vext_in = copy(before_y, vext.at[first, edge_sent], vext_far.at[:, edge_sent], last_y, after_y)
 
     table.wait()
-    lax.fori_loop(0, per_half, place, 0, unroll=2)
+    lax.fori_loop(0, per_half, place, 0, unroll=4)
 
     def sum_planes(first, count, unit, own):
         def body(step, carry):
@@ -243,12 +243,14 @@
     rest_in = copy(after_y, partial.at[others, far_sent], from_y.at[others, edge_sent], next_y, before_y)
     far_in, edge_in, inner_in, next_in = [], [], [], []
     for g in range(groups):
-        sum_planes(rows_x + g * GROUP, GROUP, GROUP, False)
-        far_in.append(copy(after_x, partial.at[beyond[g], far_sent], from_x.at[spans[g], far_sent], next_x, before_x))
-        edge_in.append(copy(after_x, partial.at[beyond[g], edge], from_x.at[spans[g], edge], next_x, before_x))
         sum_planes(g * GROUP, GROUP, GROUP, True)
         for rows in (far_sent, edge):
             next_in.append(copy(feeds, partial.at[spans[g], rows], from_next.at[spans[g], rows], last_x, alone))
+        sum_planes(rows_x + g * GROUP, GROUP, GROUP, False)
+        far_in.append(copy(
+            after_x, partial.at[beyond[g], far_sent], from_x.at[spans[g], far_sent], next_x, before_x))
+        edge_in.append(copy(after_x, partial.at[beyond[g], edge], from_x.at[spans[g], edge], next_x, before_x))
+
     vext_next_in = copy(feeds, vext.at[first, edge], vext_next, last_x, alone)
 
     onward_in, back_in, halo_onward_in, halo_back_in = [], [], [], []

time: 18.1 us -> 17.8 us (0.983)
  Pallas kernels: 16.7 us -> 16.4 us
    pallas_call x1, Pallas kernels: 15.5 us -> 15.2 us  [shards(): pl.pallas_call(functools.partial(kernel, (slots, rows_x, rows_y, depth, n...]
where the time goes in v8:
time: 17.8 us; the launch traced here: 17.7 us
  Pallas kernels  16.4 us (92%)
  between operations  1.29 us (7%)
    pallas_call x1, Pallas kernels, shards(): pl.pallas_call(functools.partial(kernel, (slots, rows_x, rows_y, depth, n...  15.2 us
    pallas_call x1, Pallas kernels, shards(): pl.pallas_call(deliver, out_shape=(jax.ShapeDtypeStruct(coeffs.shape, BF1...  1.16 us

profile of v8, /device:TPU:1, one launch (start us, length us, event | category | flops | bytes accessed | tf_op | source)
XLA Modules:
  0.0 17.7 jit_solution(13353970945594651457)
XLA Ops:
  1.3 15.2 %shard_map.86 = (bf16[2,256,256]{2,1,0:T(8,128)(2,1)S(1)}, bf16[2,256,256]{2,1,0:T(8,128)(2,1)S(1)}, f32[40,48,128]{2,1,0:T(8,128)S(1)}) custom-call(f32[16]{0:T(128)} %occ_hbm.1, s32[3,16]{1,0:T(4,128)} %bitcast.1, s32[1]{0:T(128)S(6)} %copy.9.live, f32[16,16]{1,0:T(8,128)} %syn_hbm.1, bf16[16,16,256]{2,1,0:T(8,128)(2,1)} %coef_hbm.1, ...), custom_call_target="tpu_custom_call" | custom-call | tf_op jit(solution)/shard_map/pallas_call | solution.py:362
  16.5 1.2 %shard_map.87 = (bf16[16,16,256]{2,1,0:T(8,128)(2,1)}, f32[24,32,128]{2,1,0:T(8,128)}) custom-call(bf16[2,256,256]{2,1,0:T(8,128)(2,1)S(1)} %get-tuple-element.5.boxes, bf16[2,256,256]{2,1,0:T(8,128)(2,1)S(1)} %get-tuple-element.6.back, f32[40,48,128]{2,1,0:T(8,128)S(1)} %get-tuple-element.7.ext), custom_call_target="tpu_custom_call" | custom-call | tf_op jit(solution)/shard_map/pallas_call | solution.py:399

commit v9 on v8

--- a/solution.py
+++ b/solution.py
@@ -33,29 +33,26 @@
     return lax.dot_general(left, right, (((1,), (0,)), ((), ())), preferred_element_type=F32)
 
 
+def swap_half(value):
+    half = EDGE // 2
+    block = iota((EDGE, 128), 1) // EDGE
+    parts = []
+    for t in range(2):
+        part = [value[p * EDGE : (p + 1) * EDGE] for p in range(t * half, (t + 1) * half)]
+        for step in (1, 2, 4):
+            there = (block & step) != 0
+            part = [
+                jnp.where(there, part[p], pltpu.roll(part[p - step], 128 - step * EDGE, 1))
+                if p & step
+                else jnp.where(there, pltpu.roll(part[p + step], step * EDGE, 1), part[p])
+                for p in range(half)
+            ]
+        parts.append(jnp.concatenate(part, axis=0))
+    return jnp.concatenate(parts, axis=1)
+
+
 def swap_blocks(value):
-    half = EDGE // 2
-    tiles = [
-        [[value[p * EDGE : (p + 1) * EDGE, t * 128 : (t + 1) * 128] for p in range(u * half, (u + 1) * half)] for t in range(2)]
-        for u in range(2)
-    ]
-    block = iota((EDGE, 128), 1) // EDGE
-    rows = []
-    for u in range(2):
-        parts = []
-        for t in range(2):
-            part = tiles[t][u]
-            for step in (1, 2, 4):
-                there = (block & step) != 0
-                part = [
-                    jnp.where(there, part[p], pltpu.roll(part[p - step], 128 - step * EDGE, 1))
-                    if p & step
-                    else jnp.where(there, pltpu.roll(part[p + step], step * EDGE, 1), part[p])
-                    for p in range(half)
-                ]
-            parts.append(jnp.concatenate(part, axis=0))
-        rows.append(jnp.concatenate(parts, axis=1))
-    return jnp.concatenate(rows, axis=0)
+    return jnp.concatenate([swap_half(value[:, :128]), swap_half(value[:, 128:])], axis=0)
 
 
 def kernel(
@@ -342,13 +339,17 @@
     rows_x, rows_y, _ = pot_hbm.shape
     pot_out = pltpu.make_async_copy(ext.at[pl.ds(0, rows_x), pl.ds(0, rows_y)], pot_hbm, sems.at[0])
     pot_out.start()
-    high, low = boxes[0], boxes[1]
-    result = dot(back[0], high) + (dot(back[0], low) + dot(back[1], high))
-    hpsi[...] = swap_blocks(result).astype(BF16).reshape(slots, EDGE, CUBE)
-    hpsi_out = pltpu.make_async_copy(hpsi, hpsi_hbm, sems.at[1])
-    hpsi_out.start()
-    pot_out.wait()
-    hpsi_out.wait()
+    outs = [pot_out]
+    for half in range(2):
+        lanes, part = slice(half * 128, (half + 1) * 128), pl.ds(half * slots // 2, slots // 2)
+        high, low = boxes[0, :, lanes], boxes[1, :, lanes]
+        result = dot(back[0], high) + (dot(back[0], low) + dot(back[1], high))
+        hpsi[part] = swap_half(result).astype(BF16).reshape(slots // 2, EDGE, CUBE)
+        out = pltpu.make_async_copy(hpsi.at[part], hpsi_hbm.at[part], sems.at[1 + half])
+        out.start()
+        outs.append(out)
+    for out in outs:
+        out.wait()
 
 
 def shards(n_gx, n_yz, coeffs, occupation, box_offset, live_count, synthesis, v_ext, core_density):
@@ -401,7 +402,7 @@
         out_shape=(jax.ShapeDtypeStruct(coeffs.shape, BF16), jax.ShapeDtypeStruct(v_ext.shape, F32)),
         in_specs=[vmem, vmem, vmem],
         out_specs=(hbm, hbm),
-        scratch_shapes=[pltpu.VMEM(coeffs.shape, BF16), pltpu.SemaphoreType.DMA((2,))],
+        scratch_shapes=[pltpu.VMEM(coeffs.shape, BF16), pltpu.SemaphoreType.DMA((3,))],
         compiler_params=pltpu.CompilerParams(vmem_limit_bytes=16 * 1024 * 1024),
     )(boxes, back, ext)
 

time: 17.8 us -> 17.9 us (level)
  no operation moved by 1% of the time
where the time goes in v9:
time: 17.9 us; the launch traced here: 17.8 us
  Pallas kernels  16.5 us (92%)
  between operations  1.29 us (7%)
    pallas_call x1, Pallas kernels, shards(): pl.pallas_call(functools.partial(kernel, (slots, rows_x, rows_y, depth, n...  15.2 us
    pallas_call x1, Pallas kernels, shards(): pl.pallas_call(deliver, out_shape=(jax.ShapeDtypeStruct(coeffs.shape, BF1...  1.23 us

profile of v9, /device:TPU:1, one launch (start us, length us, event | category | flops | bytes accessed | tf_op | source)
XLA Modules:
  0.0 17.8 jit_solution(185625110844771478)
XLA Ops:
  1.3 15.2 %shard_map.86 = (bf16[2,256,256]{2,1,0:T(8,128)(2,1)S(1)}, bf16[2,256,256]{2,1,0:T(8,128)(2,1)S(1)}, f32[40,48,128]{2,1,0:T(8,128)S(1)}) custom-call(f32[16]{0:T(128)} %occ_hbm.1, s32[3,16]{1,0:T(4,128)} %bitcast.1, s32[1]{0:T(128)S(6)} %copy.9.live, f32[16,16]{1,0:T(8,128)} %syn_hbm.1, bf16[16,16,256]{2,1,0:T(8,128)(2,1)} %coef_hbm.1, ...), custom_call_target="tpu_custom_call" | custom-call | tf_op jit(solution)/shard_map/pallas_call | solution.py:363
  16.5 1.2 %shard_map.87 = (bf16[16,16,256]{2,1,0:T(8,128)(2,1)}, f32[24,32,128]{2,1,0:T(8,128)}) custom-call(bf16[2,256,256]{2,1,0:T(8,128)(2,1)S(1)} %get-tuple-element.5.boxes, bf16[2,256,256]{2,1,0:T(8,128)(2,1)S(1)} %get-tuple-element.6.back, f32[40,48,128]{2,1,0:T(8,128)S(1)} %get-tuple-element.7.ext), custom_call_target="tpu_custom_call" | custom-call | tf_op jit(solution)/shard_map/pallas_call | solution.py:400

commit v10 on v8

--- a/solution.py
+++ b/solution.py
@@ -239,13 +239,14 @@
         lax.fori_loop(0, count // unit, body, 0)
 
     load_core.wait()
-    sum_planes(REACH, rest, 3, True)
-    rest_in = copy(after_y, partial.at[others, far_sent], from_y.at[others, edge_sent], next_y, before_y)
     far_in, edge_in, inner_in, next_in = [], [], [], []
     for g in range(groups):
         sum_planes(g * GROUP, GROUP, GROUP, True)
         for rows in (far_sent, edge):
             next_in.append(copy(feeds, partial.at[spans[g], rows], from_next.at[spans[g], rows], last_x, alone))
+        if g == 0:
+            sum_planes(REACH, rest, 3, True)
+            rest_in = copy(after_y, partial.at[others, far_sent], from_y.at[others, edge_sent], next_y, before_y)
         sum_planes(rows_x + g * GROUP, GROUP, GROUP, False)
         far_in.append(copy(
             after_x, partial.at[beyond[g], far_sent], from_x.at[spans[g], far_sent], next_x, before_x))

time: 17.8 us -> 17.8 us (level)
  no operation moved by 1% of the time
where the time goes in v10:
time: 17.8 us; the launch traced here: 17.7 us
  Pallas kernels  16.4 us (92%)
  between operations  1.29 us (7%)
    pallas_call x1, Pallas kernels, shards(): pl.pallas_call(functools.partial(kernel, (slots, rows_x, rows_y, depth, n...  15.2 us
    pallas_call x1, Pallas kernels, shards(): pl.pallas_call(deliver, out_shape=(jax.ShapeDtypeStruct(coeffs.shape, BF1...  1.16 us

profile of v10, /device:TPU:1, one launch (start us, length us, event | category | flops | bytes accessed | tf_op | source)
XLA Modules:
  0.0 17.7 jit_solution(6729639483695993776)
XLA Ops:
  1.3 15.2 %shard_map.86 = (bf16[2,256,256]{2,1,0:T(8,128)(2,1)S(1)}, bf16[2,256,256]{2,1,0:T(8,128)(2,1)S(1)}, f32[40,48,128]{2,1,0:T(8,128)S(1)}) custom-call(f32[16]{0:T(128)} %occ_hbm.1, s32[3,16]{1,0:T(4,128)} %bitcast.1, s32[1]{0:T(128)S(6)} %copy.9.live, f32[16,16]{1,0:T(8,128)} %syn_hbm.1, bf16[16,16,256]{2,1,0:T(8,128)(2,1)} %coef_hbm.1, ...), custom_call_target="tpu_custom_call" | custom-call | tf_op jit(solution)/shard_map/pallas_call | solution.py:363
  16.5 1.2 %shard_map.87 = (bf16[16,16,256]{2,1,0:T(8,128)(2,1)}, f32[24,32,128]{2,1,0:T(8,128)}) custom-call(bf16[2,256,256]{2,1,0:T(8,128)(2,1)S(1)} %get-tuple-element.5.boxes, bf16[2,256,256]{2,1,0:T(8,128)(2,1)S(1)} %get-tuple-element.6.back, f32[40,48,128]{2,1,0:T(8,128)S(1)} %get-tuple-element.7.ext), custom_call_target="tpu_custom_call" | custom-call | tf_op jit(solution)/shard_map/pallas_call | solution.py:400
